TPU v7x, 32 devices: a whole 2x2x4 slice. The times are simulated.
32 devices in a mesh: dp: 8 (over z, x), mp: 4 (over y, core).
Axes of the slice: x: 2, y: 2, z: 4, core: 2. Of those that a mesh axis runs over, the one named last changes fastest.
Arguments:
- tokens: bfloat16 [8192, 768], P(('dp', 'mp')), may hold values from -6 to 6
- cotangent: float32 [8192, 768], P(('dp', 'mp')), may hold values from -6 to 6
- lengths: int32 [8, 8], P('dp'), may hold values from 1 to 896, 1024 in all within a row
- key_mask: int32 [8192], P('dp'), may hold values 0 or 1
- qkv_weight: float32 [2, 768, 2304], P(None, 'dp'), may hold values from -0.21875 to 0.21875
- qkv_first: float32 [2, 768, 2304], P(None, 'dp'), may hold values from -768 to 768
- qkv_second: float32 [2, 768, 2304], P(None, 'dp'), may hold values from 18432 to 73728
- qkv_average: float32 [2, 768, 2304], P(None, 'dp'), may hold values from -0.21875 to 0.21875
- out_weight: float32 [2, 768, 768], P(None, 'dp'), may hold values from -4 to 4
- out_first: float32 [2, 768, 768], P(None, 'dp'), may hold values from -48 to 48
- out_second: float32 [2, 768, 768], P(None, 'dp'), may hold values from 66.3552 to 265.4208
- out_average: float32 [2, 768, 768], P(None, 'dp'), may hold values from -4 to 4
- gate_up_weight: float32 [2, 768, 2, 3072], P(None, 'dp', None, 'mp'), may hold values from -0.21875 to 0.21875
- gate_up_first: float32 [2, 768, 2, 3072], P(None, 'dp', None, 'mp'), may hold values from -160 to 160
- gate_up_second: float32 [2, 768, 2, 3072], P(None, 'dp', None, 'mp'), may hold values from 737.28 to 2949.12
- gate_up_average: float32 [2, 768, 2, 3072], P(None, 'dp', None, 'mp'), may hold values from -0.21875 to 0.21875
- down_weight: float32 [2, 768, 3072], P(None, 'dp', 'mp'), may hold values from -0.109375 to 0.109375
- down_first: float32 [2, 768, 3072], P(None, 'dp', 'mp'), may hold values from -448 to 448
- down_second: float32 [2, 768, 3072], P(None, 'dp', 'mp'), may hold values from 5242.88 to 20971.52
- down_average: float32 [2, 768, 3072], P(None, 'dp', 'mp'), may hold values from -0.109375 to 0.109375
- norm_gain: float32 [2, 2, 768], P(None, None, 'dp'), may hold values from 0.5 to 1.5
- gain_first: float32 [2, 2, 768], P(None, None, 'dp'), may hold values from -768 to 768
- gain_second: float32 [2, 2, 768], P(None, None, 'dp'), may hold values from 18432 to 73728
- gain_average: float32 [2, 2, 768], P(None, None, 'dp'), may hold values from 0.5 to 1.5
Outputs:
- activations: bfloat16 [8192, 768], P(('dp', 'mp'))
- input_grad: float32 [8192, 768], P(('dp', 'mp'))
- qkv_grad: float32 [2, 768, 2304], P(None, 'dp')
- qkv_first_new: float32 [2, 768, 2304], P(None, 'dp')
- qkv_second_new: float32 [2, 768, 2304], P(None, 'dp')
- qkv_new: float32 [2, 768, 2304], P(None, 'dp')
- qkv_average_new: float32 [2, 768, 2304], P(None, 'dp')
- out_grad: float32 [2, 768, 768], P(None, 'dp')
- out_first_new: float32 [2, 768, 768], P(None, 'dp')
- out_second_new: float32 [2, 768, 768], P(None, 'dp')
- out_new: float32 [2, 768, 768], P(None, 'dp')
- out_average_new: float32 [2, 768, 768], P(None, 'dp')
- gate_up_grad: float32 [2, 768, 2, 3072], P(None, 'dp', None, 'mp')
- gate_up_first_new: float32 [2, 768, 2, 3072], P(None, 'dp', None, 'mp')
- gate_up_second_new: float32 [2, 768, 2, 3072], P(None, 'dp', None, 'mp')
- gate_up_new: float32 [2, 768, 2, 3072], P(None, 'dp', None, 'mp')
- gate_up_average_new: float32 [2, 768, 2, 3072], P(None, 'dp', None, 'mp')
- down_grad: float32 [2, 768, 3072], P(None, 'dp', 'mp')
- down_first_new: float32 [2, 768, 3072], P(None, 'dp', 'mp')
- down_second_new: float32 [2, 768, 3072], P(None, 'dp', 'mp')
- down_new: float32 [2, 768, 3072], P(None, 'dp', 'mp')
- down_average_new: float32 [2, 768, 3072], P(None, 'dp', 'mp')
- gain_grad: float32 [2, 2, 768], P(None, None, 'dp')
- gain_first_new: float32 [2, 2, 768], P(None, None, 'dp')
- gain_second_new: float32 [2, 2, 768], P(None, None, 'dp')
- gain_new: float32 [2, 2, 768], P(None, None, 'dp')
- gain_average_new: float32 [2, 2, 768], P(None, None, 'dp')
Inputs may be any that keep to these rules, and one draw needn't show every extreme that they name: Row p lists the lengths of the 8 documents of pack p in order; they sum to 1024.
All inputs are finite; a program needn't handle non-finite values. No bound on the sum of `key_mask` on one device may be relied on, other than what follows from the above.
Results may differ from a plain program's by a relative error of at most 0.03.
Values may be sent and summed in bfloat16 or wider, within the bound.
A program may use at most 192 MiB of HBM per device.

v0:
```python
import jax
import jax.numpy as jnp
from jax import lax
from jax.sharding import PartitionSpec as P

HEADS = 12
HEAD_DIM = 64
LAYERS = 2
STEP = 10


rotary_base = 1000.0
norm_epsilon = 1e-05
masked_score = -1e30
beta_first = 0.5
beta_second = 0.5
adam_epsilon = 1e-08
average_decay = 0.5


def pack_layout(length_row, mask_row):
    seq_len = mask_row.shape[0]
    doc_count = length_row.shape[0]
    ends = jnp.cumsum(length_row)
    starts = ends - length_row
    spots = jnp.arange(seq_len, dtype=jnp.int32)
    member = jnp.logical_and(spots[:, None] >= starts[None, :], spots[:, None] < ends[None, :])
    doc_number = jnp.sum(
        jnp.where(member, jnp.arange(doc_count, dtype=jnp.int32)[None, :], 0), axis=1
    )
    position = spots - jnp.sum(jnp.where(member, starts[None, :], 0), axis=1)
    same_doc = doc_number[:, None] == doc_number[None, :]
    visible = jnp.logical_or(mask_row[None, :] == 1, spots[:, None] == spots[None, :])
    return (jnp.logical_and(same_doc, visible), position)


def rotary_tables(position):
    half = HEAD_DIM // 2
    freq = jnp.power(rotary_base, -2.0 * jnp.arange(half).astype(jnp.float32) / HEAD_DIM)
    angle = position.astype(jnp.float32)[..., None] * freq
    return (jnp.cos(angle), jnp.sin(angle))


def rotate(block, cos_rows, sin_rows):
    half = block.shape[-1] // 2
    front = block[..., :half]
    back_half = block[..., half:]
    cos_wide = cos_rows[..., None, :]
    sin_wide = sin_rows[..., None, :]
    return jnp.concatenate(
        [front * cos_wide - back_half * sin_wide, back_half * cos_wide + front * sin_wide], axis=-1
    )


def rotate_back(block, cos_rows, sin_rows):
    half = block.shape[-1] // 2
    front = block[..., :half]
    back_half = block[..., half:]
    cos_wide = cos_rows[..., None, :]
    sin_wide = sin_rows[..., None, :]
    return jnp.concatenate(
        [front * cos_wide + back_half * sin_wide, back_half * cos_wide - front * sin_wide], axis=-1
    )


def norm_forward(rows, gain):
    centered = rows - jnp.mean(rows, axis=-1, keepdims=True)
    inverse = lax.rsqrt(jnp.mean(centered * centered, axis=-1, keepdims=True) + norm_epsilon)
    normed = centered * inverse
    return (normed * gain, normed, inverse)


def norm_backward(grad_out, normed, inverse, gain):
    scaled = grad_out * gain
    grad_rows = (
        scaled
        - jnp.mean(scaled, axis=-1, keepdims=True)
        - normed * jnp.mean(scaled * normed, axis=-1, keepdims=True)
    ) * inverse
    return (grad_rows, jnp.sum(grad_out * normed, axis=0))


def attention_forward(query, key_rows, value_rows, allowed):
    seq_len = query.shape[0]
    scale = HEAD_DIM ** (-0.5)

    def one_head(parts):
        head_query, head_keys, head_values = parts
        scores = (
            lax.dot_general(
                head_query, head_keys, (((1,), (1,)), ((), ())), preferred_element_type=jnp.float32
            )
            * scale
        )
        scores = jnp.where(allowed, scores, masked_score)
        top = jnp.max(scores, axis=1, keepdims=True)
        weights = jnp.exp(scores - top)
        total = jnp.sum(weights, axis=1, keepdims=True)
        probs = (weights / total).astype(jnp.bfloat16)
        result = jnp.dot(probs, head_values, preferred_element_type=jnp.float32)
        return (result.astype(jnp.bfloat16), (top + jnp.log(total))[:, 0])

    outs, log_total = lax.map(
        one_head,
        (query.transpose(1, 0, 2), key_rows.transpose(1, 0, 2), value_rows.transpose(1, 0, 2)),
    )
    return (outs.transpose(1, 0, 2).reshape(seq_len, HEADS * HEAD_DIM), log_total)


def attention_backward(query, key_rows, value_rows, log_total, grad_att, allowed):
    scale = HEAD_DIM ** (-0.5)

    def one_head(parts):
        head_query, head_keys, head_values, head_total, head_grad = parts
        scores = (
            lax.dot_general(
                head_query, head_keys, (((1,), (1,)), ((), ())), preferred_element_type=jnp.float32
            )
            * scale
        )
        probs = jnp.where(allowed, jnp.exp(scores - head_total[:, None]), 0.0)
        grad_probs = lax.dot_general(
            head_grad, head_values, (((1,), (1,)), ((), ())), preferred_element_type=jnp.float32
        )
        delta = jnp.sum(probs * grad_probs, axis=1, keepdims=True)
        grad_scores = (probs * (grad_probs - delta)).astype(jnp.bfloat16)
        grad_query = jnp.dot(grad_scores, head_keys, preferred_element_type=jnp.float32) * scale
        grad_keys = (
            lax.dot_general(
                grad_scores,
                head_query,
                (((0,), (0,)), ((), ())),
                preferred_element_type=jnp.float32,
            )
            * scale
        )
        grad_values = lax.dot_general(
            probs.astype(jnp.bfloat16),
            head_grad,
            (((0,), (0,)), ((), ())),
            preferred_element_type=jnp.float32,
        )
        return (grad_query, grad_keys, grad_values)

    parts = (
        query.transpose(1, 0, 2),
        key_rows.transpose(1, 0, 2),
        value_rows.transpose(1, 0, 2),
        log_total,
        grad_att.transpose(1, 0, 2),
    )
    grad_query, grad_keys, grad_values = lax.map(one_head, parts)
    return (
        grad_query.transpose(1, 0, 2),
        grad_keys.transpose(1, 0, 2),
        grad_values.transpose(1, 0, 2),
    )


def layer_forward(layer_rows, gathered, gain_pair, allowed, cos_rows, sin_rows, offset):
    qkv_full, out_full, gate_up_local, down_local = gathered
    rows_own = layer_rows.shape[0]
    rows_full = lax.all_gather(layer_rows, "mp", axis=0, tiled=True)
    seq_len = rows_full.shape[0]
    proj = jnp.dot(rows_full, qkv_full, preferred_element_type=jnp.float32)
    split_heads = proj.reshape(seq_len, 3, HEADS, HEAD_DIM)
    query = rotate(split_heads[:, 0], cos_rows, sin_rows).astype(jnp.bfloat16)
    key_rows = rotate(split_heads[:, 1], cos_rows, sin_rows).astype(jnp.bfloat16)
    value_rows = split_heads[:, 2].astype(jnp.bfloat16)
    att_out, log_total = attention_forward(query, key_rows, value_rows, allowed)
    branch = jnp.dot(att_out, out_full, preferred_element_type=jnp.float32)
    first_out, first_normed, first_inverse = norm_forward(
        rows_full.astype(jnp.float32) + branch, gain_pair[0]
    )
    first_low = first_out.astype(jnp.bfloat16)
    gate_up = jnp.einsum(
        "sd,dkf->skf", first_low, gate_up_local, preferred_element_type=jnp.float32
    )
    hidden = (jax.nn.silu(gate_up[:, 0]) * gate_up[:, 1]).astype(jnp.bfloat16)
    ffn_own = lax.psum_scatter(
        lax.dot_general(
            hidden, down_local, (((1,), (1,)), ((), ())), preferred_element_type=jnp.float32
        ).astype(jnp.bfloat16),
        "mp",
        scatter_dimension=0,
        tiled=True,
    ).astype(jnp.float32)
    first_own = lax.dynamic_slice_in_dim(first_out, offset, rows_own, 0)
    result, second_normed, second_inverse = norm_forward(first_own + ffn_own, gain_pair[1])
    kept = (
        rows_full,
        query,
        key_rows,
        value_rows,
        log_total,
        att_out,
        lax.dynamic_slice_in_dim(first_normed, offset, rows_own, 0),
        lax.dynamic_slice_in_dim(first_inverse, offset, rows_own, 0),
        first_low,
        gate_up,
        hidden,
        second_normed,
        second_inverse,
    )
    return (result.astype(jnp.bfloat16), kept)


def layer_backward(grad_own, gathered, gain_pair, kept, allowed, cos_rows, sin_rows, offset):
    qkv_full, out_full, gate_up_local, down_local = gathered
    (
        rows_full,
        query,
        key_rows,
        value_rows,
        log_total,
        att_out,
        first_normed,
        first_inverse,
        first_low,
        gate_up,
        hidden,
        second_normed,
        second_inverse,
    ) = kept
    rows_own = grad_own.shape[0]
    seq_len = rows_full.shape[0]
    grad_sum_rows, second_gain = norm_backward(
        grad_own, second_normed, second_inverse, gain_pair[1]
    )
    ffn_grad = lax.all_gather(grad_sum_rows.astype(jnp.bfloat16), "mp", axis=0, tiled=True)
    grad_hidden = jnp.dot(ffn_grad, down_local, preferred_element_type=jnp.float32)
    grad_down = lax.dot_general(
        ffn_grad, hidden, (((0,), (0,)), ((), ())), preferred_element_type=jnp.float32
    )
    gate = gate_up[:, 0]
    upward = gate_up[:, 1]
    sigma = jax.nn.sigmoid(gate)
    grad_gate = grad_hidden * upward * sigma * (1.0 + gate * (1.0 - sigma))
    grad_upward = grad_hidden * gate * sigma
    grad_gate_up = jnp.stack([grad_gate, grad_upward], axis=1).astype(jnp.bfloat16)
    grad_gate_up_weight = jnp.einsum(
        "sd,skf->dkf", first_low, grad_gate_up, preferred_element_type=jnp.float32
    )
    grad_first = (
        lax.psum_scatter(
            jnp.einsum(
                "skf,dkf->sd", grad_gate_up, gate_up_local, preferred_element_type=jnp.float32
            ).astype(jnp.bfloat16),
            "mp",
            scatter_dimension=0,
            tiled=True,
        ).astype(jnp.float32)
        + grad_sum_rows
    )
    grad_resid, first_gain = norm_backward(grad_first, first_normed, first_inverse, gain_pair[0])
    branch_grad = lax.all_gather(grad_resid.astype(jnp.bfloat16), "mp", axis=0, tiled=True)
    grad_att = lax.dot_general(
        branch_grad, out_full, (((1,), (1,)), ((), ())), preferred_element_type=jnp.float32
    )
    grad_att = grad_att.astype(jnp.bfloat16).reshape(seq_len, HEADS, HEAD_DIM)
    grad_query, grad_keys, grad_values = attention_backward(
        query, key_rows, value_rows, log_total, grad_att, allowed
    )
    grad_proj = jnp.stack(
        [
            rotate_back(grad_query, cos_rows, sin_rows),
            rotate_back(grad_keys, cos_rows, sin_rows),
            grad_values,
        ],
        axis=1,
    )
    grad_proj = grad_proj.reshape(seq_len, 3 * HEADS * HEAD_DIM).astype(jnp.bfloat16)
    grad_qkv = lax.dot_general(
        rows_full, grad_proj, (((0,), (0,)), ((), ())), preferred_element_type=jnp.float32
    )
    grad_out = lax.dot_general(
        att_out, branch_grad, (((0,), (0,)), ((), ())), preferred_element_type=jnp.float32
    )
    proj_own = lax.dynamic_slice_in_dim(grad_proj, offset, rows_own, 0)
    grad_input = grad_resid + lax.dot_general(
        proj_own, qkv_full, (((1,), (1,)), ((), ())), preferred_element_type=jnp.float32
    )
    return (
        grad_input,
        (grad_qkv, grad_out, grad_gate_up_weight, grad_down),
        jnp.stack([first_gain, second_gain]),
    )


def adamw(weight, first, second, average, gradient, rate, decay):
    first_new = beta_first * first + (1.0 - beta_first) * gradient
    second_new = beta_second * second + (1.0 - beta_second) * gradient * gradient
    first_hat = first_new / (1.0 - beta_first**STEP)
    second_hat = second_new / (1.0 - beta_second**STEP)
    weight_new = weight - rate * (
        first_hat / (jnp.sqrt(second_hat) + adam_epsilon) + decay * weight
    )
    average_new = average_decay * average + (1.0 - average_decay) * weight_new
    return (gradient, first_new, second_new, weight_new, average_new)


def shards(
    tokens,
    cotangent,
    lengths,
    key_mask,
    qkv_weight,
    qkv_first,
    qkv_second,
    qkv_average,
    out_weight,
    out_first,
    out_second,
    out_average,
    gate_up_weight,
    gate_up_first,
    gate_up_second,
    gate_up_average,
    down_weight,
    down_first,
    down_second,
    down_average,
    norm_gain,
    gain_first,
    gain_second,
    gain_average,
):
    rows_own = tokens.shape[0]
    offset = lax.axis_index("mp") * rows_own
    gain_full = lax.all_gather(norm_gain, "dp", axis=2, tiled=True)
    allowed, position = pack_layout(lengths[0], key_mask)
    cos_rows, sin_rows = rotary_tables(position)
    layer_rows = tokens
    kept_all = []
    gathered_all = []
    for layer in range(LAYERS):
        gathered = (
            lax.all_gather(qkv_weight[layer].astype(jnp.bfloat16), "dp", axis=0, tiled=True),
            lax.all_gather(out_weight[layer].astype(jnp.bfloat16), "dp", axis=0, tiled=True),
            lax.all_gather(gate_up_weight[layer].astype(jnp.bfloat16), "dp", axis=0, tiled=True),
            lax.all_gather(down_weight[layer].astype(jnp.bfloat16), "dp", axis=0, tiled=True),
        )
        layer_rows, kept = layer_forward(
            layer_rows, gathered, gain_full[layer], allowed, cos_rows, sin_rows, offset
        )
        kept_all.append(kept)
        gathered_all.append(None)
    grad_rows = cotangent
    weight_parts = [None] * LAYERS
    gain_parts = [None] * LAYERS
    for layer in range(LAYERS - 1, -1, -1):
        gathered = (
            lax.all_gather(qkv_weight[layer].astype(jnp.bfloat16), "dp", axis=0, tiled=True),
            lax.all_gather(out_weight[layer].astype(jnp.bfloat16), "dp", axis=0, tiled=True),
            lax.all_gather(gate_up_weight[layer].astype(jnp.bfloat16), "dp", axis=0, tiled=True),
            lax.all_gather(down_weight[layer].astype(jnp.bfloat16), "dp", axis=0, tiled=True),
        )
        grad_rows, layer_grads, gain_parts[layer] = layer_backward(
            grad_rows,
            gathered,
            gain_full[layer],
            kept_all[layer],
            allowed,
            cos_rows,
            sin_rows,
            offset,
        )
        weight_parts[layer] = (
            lax.psum_scatter(layer_grads[0], "dp", scatter_dimension=0, tiled=True),
            lax.psum_scatter(layer_grads[1], "dp", scatter_dimension=0, tiled=True),
            lax.psum_scatter(layer_grads[2], "dp", scatter_dimension=0, tiled=True),
            lax.psum_scatter(layer_grads[3], "dp", scatter_dimension=0, tiled=True),
        )
    stacked = [
        jnp.stack([weight_parts[layer][member] for layer in range(LAYERS)]) for member in range(4)
    ]
    stacked = list(stacked)
    gain_pack = lax.psum(jnp.stack(gain_parts), "mp")
    gain_grad = lax.psum_scatter(gain_pack, "dp", scatter_dimension=2, tiled=True)
    results = [layer_rows, grad_rows]
    results.extend(adamw(qkv_weight, qkv_first, qkv_second, qkv_average, stacked[0], 0.03, 0.01))
    results.extend(adamw(out_weight, out_first, out_second, out_average, stacked[1], 0.5, 0.01))
    results.extend(
        adamw(
            gate_up_weight, gate_up_first, gate_up_second, gate_up_average, stacked[2], 0.03, 0.01
        )
    )
    results.extend(
        adamw(down_weight, down_first, down_second, down_average, stacked[3], 0.02, 0.01)
    )
    results.extend(adamw(norm_gain, gain_first, gain_second, gain_average, gain_grad, 0.6, 0.0))
    return tuple(results)


def solution(mesh):
    return jax.shard_map(
        shards,
        mesh=mesh,
        in_specs=(
            P(("dp", "mp"), None),
            P(("dp", "mp"), None),
            P("dp", None),
            P("dp"),
            P(None, "dp", None),
            P(None, "dp", None),
            P(None, "dp", None),
            P(None, "dp", None),
            P(None, "dp", None),
            P(None, "dp", None),
            P(None, "dp", None),
            P(None, "dp", None),
            P(None, "dp", None, "mp"),
            P(None, "dp", None, "mp"),
            P(None, "dp", None, "mp"),
            P(None, "dp", None, "mp"),
            P(None, "dp", "mp"),
            P(None, "dp", "mp"),
            P(None, "dp", "mp"),
            P(None, "dp", "mp"),
            P(None, None, "dp"),
            P(None, None, "dp"),
            P(None, None, "dp"),
            P(None, None, "dp"),
        ),
        out_specs=(
            P(("dp", "mp"), None),
            P(("dp", "mp"), None),
            P(None, "dp", None),
            P(None, "dp", None),
            P(None, "dp", None),
            P(None, "dp", None),
            P(None, "dp", None),
            P(None, "dp", None),
            P(None, "dp", None),
            P(None, "dp", None),
            P(None, "dp", None),
            P(None, "dp", None),
            P(None, "dp", None, "mp"),
            P(None, "dp", None, "mp"),
            P(None, "dp", None, "mp"),
            P(None, "dp", None, "mp"),
            P(None, "dp", None, "mp"),
            P(None, "dp", "mp"),
            P(None, "dp", "mp"),
            P(None, "dp", "mp"),
            P(None, "dp", "mp"),
            P(None, "dp", "mp"),
            P(None, None, "dp"),
            P(None, None, "dp"),
            P(None, None, "dp"),
            P(None, None, "dp"),
            P(None, None, "dp"),
        ),
        check_vma=False,
    )
```

profile of v0, /device:TPU:0, one launch (start us, length us, event | category | flops | bytes accessed | tf_op | source)
XLA Modules:
  0.0 1735.2 jit_solution(8821860784072530675)
XLA Ops:
  15.2 34.2 %all_gather.56 = f32[2,2,768]{1,0,2:T(2,128)S(1)} all-gather(f32[2,2,96]{1,0,2:T(2,128)S(1)} %copy.314), channel_id=1, replica_groups=mesh['dp'=8,'mp'=4] {'dp'}, dimensions={2}, use_global_device_ids=true | all-gather | bytes 13824 | tf_op jit(solution)/shard_map/all_gather | solution.py:330
  49.3 9.7 slice_reduce_fusion
  59.6 41.1 %all-gather.35.cloned.1.call-done = bf16[1,768,2304]{2,1,0:T(8,128)(2,1)} async-done(((bf16[1,96,2304]{2,1,0:T(8,128)(2,1)}), bf16[1,768,2304]{2,1,0:T(8,128)(2,1)}) %all-gather.35.cloned.1.call-update) | async-done | bytes 3538960 | tf_op jit(solution)/shard_map/all_gather | solution.py:338
  100.7 6.8 fusion.112
  125.7 113.6 %while.56 = (s32[]{:T(128)}, bf16[12,1024,64]{1,2,0:T(8,128)(2,1)}, f32[12,1024]{1,0:T(8,128)S(1)}, bf16[12,1024,64]{2,1,0:T(8,128)(2,1)S(1)}, bf16[12,1024,64]{...) while((s32[]{:T(128)}, bf16[12,1024,64]{1,2,0:T(8,128)(2,1)}, ...), condition=%wide.region_6.7_spmd.clone, body=%wide.region_3.6_spmd.clone.sunk | while | flops 281082880 | bytes 30329988 | solution.py:103
  262.1 26.1 %reduce-scatter.20.cloned.1.call-done = bf16[256,768]{0,1:T(8,128)(2,1)} async-done(((bf16[1024,768]{0,1:T(8,128)(2,1)}), bf16[256,768]{0,1:T(8,128)(2,1)}) %reduce-scatter.20.cloned.1.call-update) | async-done | bytes 393232 | tf_op jit(solution)/shard_map/reduce_scatter | solution.py:180
  293.3 12.2 reduce-scatter.22.cloned.1.call-start
  305.5 50.9 %all-gather.43.cloned.1.call-done = bf16[1,768,2304]{2,1,0:T(8,128)(2,1)} async-done(((bf16[1,96,2304]{2,1,0:T(8,128)(2,1)}), bf16[1,768,2304]{2,1,0:T(8,128)(2,1)}) %all-gather.43.cloned.1.call-update) | async-done | bytes 3538960 | tf_op jit(solution)/shard_map/all_gather | solution.py:338
  356.4 20.6 %all-gather.25.cloned.1.call-done = bf16[1024,768]{0,1:T(8,128)(2,1)} async-done(((bf16[256,768]{0,1:T(8,128)(2,1)}), bf16[1024,768]{0,1:T(8,128)(2,1)}) %all-gather.25.cloned.1.call-update) | async-done | bytes 1572880 | tf_op jit(solution)/shard_map/all_gather | solution.py:163
  377.0 6.5 fusion.108
  404.8 103.1 %while.57 = (s32[]{:T(128)}, bf16[12,1024,64]{1,2,0:T(8,128)(2,1)}, f32[12,1024]{1,0:T(8,128)S(1)}, bf16[12,1024,64]{2,1,0:T(8,128)(2,1)}, bf16[12,1024,64]{2,1,...) while((s32[]{:T(128)}, bf16[12,1024,64]{1,2,0:T(8,128)(2,1)}, ...), condition=%wide.region_15.16_spmd.clone, body=%wide.region_12.15_spmd.clone.sunk | while | flops 281082880 | bytes 30329988 | solution.py:103
  515.4 6.4 fusion.116
  533.1 26.1 %reduce-scatter.22.cloned.1.call-done = bf16[256,768]{0,1:T(8,128)(2,1)} async-done(((bf16[1024,768]{0,1:T(8,128)(2,1)}), bf16[256,768]{0,1:T(8,128)(2,1)}) %reduce-scatter.22.cloned.1.call-update) | async-done | bytes 393232 | tf_op jit(solution)/shard_map/reduce_scatter | solution.py:180
  563.2 19.5 %all-gather.27.cloned.1.call-done = bf16[1024,768]{0,1:T(8,128)(2,1)} async-done(((bf16[256,768]{0,1:T(8,128)(2,1)}), bf16[1024,768]{0,1:T(8,128)(2,1)}) %all-gather.27.cloned.1.call-update) | async-done | bytes 1572880 | tf_op jit(solution)/shard_map/all_gather | solution.py:230
  582.7 6.1 fusion.137
  594.4 28.2 %reduce-scatter.24.cloned.1.call-done = bf16[256,768]{0,1:T(8,128)(2,1)} async-done(((bf16[1024,768]{0,1:T(8,128)(2,1)}), bf16[256,768]{0,1:T(8,128)(2,1)}) %reduce-scatter.24.cloned.1.call-update) | async-done | bytes 393232 | tf_op jit(solution)/shard_map/reduce_scatter | solution.py:245
  626.6 19.7 %all-gather.29.cloned.1.call-done = bf16[1024,768]{0,1:T(8,128)(2,1)} async-done(((bf16[256,768]{0,1:T(8,128)(2,1)}), bf16[1024,768]{0,1:T(8,128)(2,1)}) %all-gather.29.cloned.1.call-update) | async-done | bytes 1572880 | tf_op jit(solution)/shard_map/all_gather | solution.py:256
  656.3 154.7 %while.58 = (s32[]{:T(128)}, f32[12,1024,64]{1,2,0:T(8,128)}, f32[12,1024,64]{1,2,0:T(8,128)}, bf16[12,1024,64]{1,2,0:T(8,128)(2,1)S(1)}, bf16[12,1024,64]{2,1,0...) while((s32[]{:T(128)}, f32[12,1024,64]{1,2,0:T(8,128)}, ...), condition=%wide.region_28.29_spmd.clone, body=%wide.region_26.28_spmd.clone.sunk | while | flops 684850176 | bytes 34113656 | solution.py:152
  823.4 19.9 %all-gather.31.cloned.1.call-done = bf16[1024,768]{0,1:T(8,128)(2,1)} async-done(((bf16[256,768]{0,1:T(8,128)(2,1)}), bf16[1024,768]{0,1:T(8,128)(2,1)}) %all-gather.31.cloned.1.call-update) | async-done | bytes 1572880 | tf_op jit(solution)/shard_map/all_gather | solution.py:230
  856.7 27.3 %reduce-scatter.26.cloned.1.call-done = bf16[256,768]{0,1:T(8,128)(2,1)} async-done(((bf16[1024,768]{0,1:T(8,128)(2,1)}), bf16[256,768]{0,1:T(8,128)(2,1)}) %reduce-scatter.26.cloned.1.call-update) | async-done | bytes 393232 | tf_op jit(solution)/shard_map/reduce_scatter | solution.py:245
  907.1 6.1 fusion.122
  925.0 8.2 fusion.198
  944.1 163.6 %while.59 = (s32[]{:T(128)}, f32[12,1024,64]{1,2,0:T(8,128)}, f32[12,1024,64]{1,2,0:T(8,128)}, bf16[12,1024,64]{1,2,0:T(8,128)(2,1)S(1)}, bf16[12,1024,64]{2,1,0...) while((s32[]{:T(128)}, f32[12,1024,64]{1,2,0:T(8,128)}, ...), condition=%wide.region_36.37_spmd.clone, body=%wide.region_34.36_spmd.clone.sunk | while | flops 684850176 | bytes 34113656 | solution.py:152
  1120.6 8.1 copy.368
  1131.6 6.3 psum.8
  1147.9 66.0 %reduce-scatter.34.cloned.1.call-done = f32[96,2,768]{2,0,1:T(8,128)} async-done(((f32[768,2,768]{2,0,1:T(8,128)}), f32[96,2,768]{2,0,1:T(8,128)}) %reduce-scatter.34.cloned.1.call-update) | async-done | bytes 589840 | tf_op jit(solution)/shard_map/reduce_scatter | solution.py:371
  1213.9 98.7 %reduce-scatter.32.cloned.1.call-done = f32[96,2,768]{2,0,1:T(8,128)} async-done(((f32[768,2,768]{2,0,1:T(8,128)}), f32[96,2,768]{2,0,1:T(8,128)}) %reduce-scatter.32.cloned.1.call-update) | async-done | bytes 589840 | tf_op jit(solution)/shard_map/reduce_scatter | solution.py:371
  1324.8 59.9 %reduce-scatter.30.cloned.1.call-done = f32[96,768]{1,0:T(8,128)} async-done(((f32[768,768]{1,0:T(8,128)}), f32[96,768]{1,0:T(8,128)}) %reduce-scatter.30.cloned.1.call-update) | async-done | bytes 294928 | tf_op jit(solution)/shard_map/reduce_scatter | solution.py:370
  1384.7 71.6 %reduce-scatter.28.cloned.1.call-done = f32[96,768]{1,0:T(8,128)} async-done(((f32[768,768]{1,0:T(8,128)}), f32[96,768]{1,0:T(8,128)}) %reduce-scatter.28.cloned.1.call-update) | async-done | bytes 294928 | tf_op jit(solution)/shard_map/reduce_scatter | solution.py:370
  1459.4 128.4 %reduce-scatter.42.cloned.1.call-done = f32[96,2304]{1,0:T(8,128)} async-done(((f32[768,2304]{1,0:T(8,128)}), f32[96,2304]{1,0:T(8,128)}) %reduce-scatter.42.cloned.1.call-update) | async-done | bytes 884752 | tf_op jit(solution)/shard_map/reduce_scatter | solution.py:369
  1587.8 132.1 %reduce-scatter.40.cloned.1.call-done = f32[96,2304]{1,0:T(8,128)} async-done(((f32[768,2304]{1,0:T(8,128)}), f32[96,2304]{1,0:T(8,128)}) %reduce-scatter.40.cloned.1.call-update) | async-done | bytes 884752 | tf_op jit(solution)/shard_map/reduce_scatter | solution.py:369
  1719.9 8.0 add_multiply_fusion
  (676 shorter events, 763.2 us)
Async XLA Ops:
  7.2 52.4 %all-gather.23.cloned.1.call-start = ((), (), s32[]{:S(2)}) async-start(), calls=%async_computation.13 | async-start | bytes 1966080 | tf_op jit(solution)/shard_map/all_gather | solution.py:163
  9.2 91.5 %all-gather.35.cloned.1.call-start = ((), (), s32[]{:S(2)}) async-start(), calls=%async_computation.29 | async-start | bytes 3981312 | tf_op jit(solution)/shard_map/all_gather | solution.py:338
  11.9 227.4 %all-gather.37.cloned.1.call-start = ((), (), s32[]{:S(2)}) async-start(), calls=%async_computation.30 | async-start | bytes 1327104 | tf_op jit(solution)/shard_map/all_gather | solution.py:339
  12.8 234.1 %all-gather.39.cloned.1.call-start = ((), (), s32[]{:S(2)}) async-start(), calls=%async_computation.31 | async-start | bytes 2654208 | tf_op jit(solution)/shard_map/all_gather | solution.py:340
  13.8 243.2 %all-gather.41.cloned.1.call-start = ((), (), s32[]{:S(2)}) async-start(), calls=%async_computation.32 | async-start | bytes 1327104 | tf_op jit(solution)/shard_map/all_gather | solution.py:341
  14.6 273.6 %reduce-scatter.20.cloned.1.call-start = ((), (), s32[]{:S(2)}) async-start(), calls=%async_computation.14 | async-start | bytes 1966080 | tf_op jit(solution)/shard_map/reduce_scatter | solution.py:180
  59.0 185.7 %copy-start.44 = (f32[768]{0:T(1024)}, f32[768]{0:T(1024)S(1)}, u32[]{:S(2)}) copy-start(f32[768]{0:T(1024)S(1)} %get-tuple-element.718) | copy-start | bytes 9220
  59.1 230.5 %copy-start.46 = (f32[768]{0:T(1024)}, f32[768]{0:T(1024)S(1)}, u32[]{:S(2)}) copy-start(f32[768]{0:T(1024)S(1)} %get-tuple-element.717) | copy-start | bytes 9220
  261.3 95.1 %all-gather.43.cloned.1.call-start = ((), (), s32[]{:S(2)}) async-start(), calls=%async_computation.33 | async-start | bytes 3981312 | tf_op jit(solution)/shard_map/all_gather | solution.py:338
  262.1 114.9 %all-gather.25.cloned.1.call-start = ((), (), s32[]{:S(2)}) async-start(), calls=%async_computation.15 | async-start | bytes 1966080 | tf_op jit(solution)/shard_map/all_gather | solution.py:163
  291.2 216.7 %all-gather.45.cloned.1.call-start = ((), (), s32[]{:S(2)}) async-start(), calls=%async_computation.34 | async-start | bytes 1327104 | tf_op jit(solution)/shard_map/all_gather | solution.py:339
  291.9 223.5 %all-gather.47.cloned.1.call-start = ((), (), s32[]{:S(2)}) async-start(), calls=%async_computation.35 | async-start | bytes 2654208 | tf_op jit(solution)/shard_map/all_gather | solution.py:340
  292.5 233.9 %all-gather.49.cloned.1.call-start = ((), (), s32[]{:S(2)}) async-start(), calls=%async_computation.36 | async-start | bytes 1327104 | tf_op jit(solution)/shard_map/all_gather | solution.py:341
  293.3 266.0 %reduce-scatter.22.cloned.1.call-start = ((), (), s32[]{:S(2)}) async-start(), calls=%async_computation.16 | async-start | bytes 1966080 | tf_op jit(solution)/shard_map/reduce_scatter | solution.py:180
  530.8 51.9 %all-gather.27.cloned.1.call-start = ((), (), s32[]{:S(2)}) async-start(), calls=%async_computation.17 | async-start | bytes 1966080 | tf_op jit(solution)/shard_map/all_gather | solution.py:230
  562.7 59.9 %reduce-scatter.24.cloned.1.call-start = ((), (), s32[]{:S(2)}) async-start(), calls=%async_computation.18 | async-start | bytes 1966080 | tf_op jit(solution)/shard_map/reduce_scatter | solution.py:245
  594.3 52.0 %all-gather.29.cloned.1.call-start = ((), (), s32[]{:S(2)}) async-start(), calls=%async_computation.19 | async-start | bytes 1966080 | tf_op jit(solution)/shard_map/all_gather | solution.py:256
  626.3 217.0 %all-gather.31.cloned.1.call-start = ((), (), s32[]{:S(2)}) async-start(), calls=%async_computation.20 | async-start | bytes 1966080 | tf_op jit(solution)/shard_map/all_gather | solution.py:230
  823.3 60.7 %reduce-scatter.26.cloned.1.call-start = ((), (), s32[]{:S(2)}) async-start(), calls=%async_computation.21 | async-start | bytes 1966080 | tf_op jit(solution)/shard_map/reduce_scatter | solution.py:245
  855.7 62.3 %all-gather.33.cloned.1.call-start = ((), (), s32[]{:S(2)}) async-start(), calls=%async_computation.22 | async-start | bytes 1966080 | tf_op jit(solution)/shard_map/all_gather | solution.py:256
  887.8 242.8 %reduce-scatter.44.cloned.1.call-start = ((), (), s32[]{:S(2)}) async-start(), calls=%async_computation.39 | async-start | bytes 442368
  889.6 248.9 %reduce-scatter.38.cloned.1.call-start = ((), (), s32[]{:S(2)}) async-start(), calls=%async_computation.28 | async-start | bytes 2654208 | tf_op jit(solution)/shard_map/reduce_scatter | solution.py:372
  893.9 244.6 %reduce-scatter.36.cloned.1.call-start = ((), (), s32[]{:S(2)}) async-start(), calls=%async_computation.27 | async-start | bytes 2654208 | tf_op jit(solution)/shard_map/reduce_scatter | solution.py:372
  899.0 314.8 %reduce-scatter.34.cloned.1.call-start = ((), (), s32[]{:S(2)}) async-start(), calls=%async_computation.26 | async-start | bytes 5308416 | tf_op jit(solution)/shard_map/reduce_scatter | solution.py:371
  905.2 407.3 %reduce-scatter.32.cloned.1.call-start = ((), (), s32[]{:S(2)}) async-start(), calls=%async_computation.25 | async-start | bytes 5308416 | tf_op jit(solution)/shard_map/reduce_scatter | solution.py:371
  913.2 471.5 %reduce-scatter.30.cloned.1.call-start = ((), (), s32[]{:S(2)}) async-start(), calls=%async_computation.24 | async-start | bytes 2654208 | tf_op jit(solution)/shard_map/reduce_scatter | solution.py:370
  918.0 538.3 %reduce-scatter.28.cloned.1.call-start = ((), (), s32[]{:S(2)}) async-start(), calls=%async_computation.23 | async-start | bytes 2654208 | tf_op jit(solution)/shard_map/reduce_scatter | solution.py:370
  923.6 664.2 %reduce-scatter.42.cloned.1.call-start = ((), (), s32[]{:S(2)}) async-start(), calls=%async_computation.38 | async-start | bytes 7962624 | tf_op jit(solution)/shard_map/reduce_scatter | solution.py:369
  933.2 786.7 %reduce-scatter.40.cloned.1.call-start = ((), (), s32[]{:S(2)}) async-start(), calls=%async_computation.37 | async-start | bytes 7962624 | tf_op jit(solution)/shard_map/reduce_scatter | solution.py:369
  1141.8 170.7 %copy-start.36 = (f32[2,96,2,768]{3,2,1,0:T(2,128)S(1)}, f32[2,96,2,768]{3,2,1,0:T(2,128)}, u32[]{:S(2)}) copy-start(f32[2,96,2,768]{3,2,1,0:T(2,128)} %param.47) | copy-start | bytes 3538948
  1141.8 170.7 %copy-start.37 = (f32[2,96,2,768]{3,2,1,0:T(2,128)S(1)}, f32[2,96,2,768]{3,2,1,0:T(2,128)}, u32[]{:S(2)}) copy-start(f32[2,96,2,768]{3,2,1,0:T(2,128)} %param.46) | copy-start | bytes 3538948
  1456.3 263.7 %copy-start.7 = (f32[2,96,2304]{2,1,0:T(8,128)S(1)}, f32[2,96,2304]{2,1,0:T(8,128)}, u32[]{:S(2)}) copy-start(f32[2,96,2304]{2,1,0:T(8,128)} %param.36) | copy-start | bytes 5308420
  (93 other events, 1297.4 us)
Sparse Core Ops, SparseCore 0:
  10.2 22.5 all-gather.22
  35.5 65.1 all-gather.34
  103.5 39.5 all-gather.36
  145.7 50.6 all-gather.38
  199.0 39.5 all-gather.40
  261.4 26.7 reduce-scatter.19
  291.2 65.1 all-gather.42
  358.6 18.3 all-gather.24
  380.0 41.0 all-gather.44
  423.9 50.8 all-gather.46
  477.8 39.5 all-gather.48
  530.9 28.2 reduce-scatter.21
  562.8 19.8 all-gather.26
  594.4 28.1 reduce-scatter.23
  626.4 19.8 all-gather.28
  823.5 19.8 all-gather.30
  855.9 28.1 reduce-scatter.25
  887.9 19.8 all-gather.32
  911.6 61.2 reduce-scatter.43
  976.3 68.0 reduce-scatter.37
  1047.9 67.9 reduce-scatter.35
  1119.5 94.2 reduce-scatter.33
  1217.5 94.9 reduce-scatter.31
  1315.9 68.7 reduce-scatter.29
  1388.2 68.0 reduce-scatter.27
  1459.8 128.0 reduce-scatter.41
  1591.8 128.0 reduce-scatter.39
where the time goes:
time: 1750 us; the launch traced here: 1740 us
  waiting for transfers between devices  839 us (48%)
  matrix products  550 us (31%)
  local copies, waits for them, and re-layouts  169 us (10%)
  other arithmetic  105 us (6%)
  blocking collectives  40.5 us (2%)
    reduce_scatter x2, waiting for transfers between devices, shards(): lax.psum_scatter(layer_grads[0], 'dp', scatter_dimension=0, tiled=True)  260 us
    reduce_scatter x2, waiting for transfers between devices, shards(): lax.psum_scatter(layer_grads[2], 'dp', scatter_dimension=0, tiled=True)  165 us
    dot_general x48, matrix products, one_head(): lax.dot_general(head_query, head_keys, (((1,), (1,)), ((), ())), preferre...  147 us
    reduce_scatter x2, waiting for transfers between devices, shards(): lax.psum_scatter(layer_grads[1], 'dp', scatter_dimension=0, tiled=True)  131 us
    all_gather x2, waiting for transfers between devices, shards(): lax.all_gather(qkv_weight[layer].astype(jnp.bfloat16), 'dp', axis=0, tile...  92 us
    dot_general x24, matrix products, one_head(): result = jnp.dot(probs, head_values, preferred_element_type=jnp.float32)  90.3 us
    unnamed x170, local copies, waits for them, and re-layouts  74.4 us
    dot_general x24, matrix products, one_head(): lax.dot_general(grad_scores, head_query, (((0,), (0,)), ((), ())), prefer...  58.3 us
  transfers between devices with their start and end apart: 27, of which 16 were waited for; matrix products, arithmetic and copies ran while one was open for 31% of the time, Pallas kernels for 0%

commit v1 on v0

v1 whole, which is shorter than its diff:
```python
import functools
import math

import jax
import jax.numpy as jnp
from jax import lax
from jax.experimental import pallas as pl
from jax.experimental.pallas import tpu as pltpu
from jax.sharding import PartitionSpec as P

HEADS = 12
HEAD_DIM = 64
LAYERS = 2
STEP = 10
GROUP = 4
OWN_HEADS = HEADS // GROUP
TILE = 2 * HEAD_DIM
PROJ = 5 * TILE

rotary_base = 1000.0
norm_epsilon = 1e-05
masked_score = -1e30
beta_first = 0.5
beta_second = 0.5
adam_epsilon = 1e-08
average_decay = 0.5
score_scale = HEAD_DIM ** (-0.5)
log2e = math.log2(math.e)

MESH = pl.DeviceIdType.MESH
ANY = pl.BlockSpec(memory_space=pl.ANY)
VMEM = pl.BlockSpec(memory_space=pltpu.VMEM)
f32 = jnp.float32
bf16 = jnp.bfloat16
VMEM_LIMIT = 127 * 2**19


def dot(a, b):
    return jnp.dot(a, b, preferred_element_type=f32)


def dot_nt(a, b):
    return lax.dot_general(a, b, (((1,), (1,)), ((), ())), preferred_element_type=f32)


def dot_tn(a, b):
    return lax.dot_general(a, b, (((0,), (0,)), ((), ())), preferred_element_type=f32)


def places():
    me = lax.axis_index("mp")
    core = lax.rem(me, 2)
    side = lax.div(me, 2)
    return me, me + 1 - 2 * core, me + 2 - 4 * side, 3 - me, core


def push(src, dst, sems, layer, number, who):
    return pltpu.make_async_remote_copy(
        src_ref=src,
        dst_ref=dst,
        send_sem=sems.at[0, layer, number],
        recv_sem=sems.at[1, layer, number],
        device_id={"mp": who},
        device_id_type=MESH,
    )


def greet(mate, across):
    barrier = pltpu.get_barrier_semaphore()
    for who in (mate, across):
        pl.semaphore_signal(barrier, inc=1, device_id={"mp": who}, device_id_type=MESH)
    pl.semaphore_wait(barrier, 2)


def rows_of(block, size, extent):
    return pl.ds(pl.multiple_of(block * size, size), extent)


def lane_iota(shape):
    return lax.broadcasted_iota(jnp.int32, shape, len(shape) - 1)


def half_masks():
    low = (lane_iota((1, TILE)) < HEAD_DIM).astype(f32)
    return low.astype(bf16), (1.0 - low).astype(bf16)


def turn(tile, cos_rows, sin_rows):
    lane = lane_iota(tile.shape) % HEAD_DIM
    half = HEAD_DIM // 2
    partner = jnp.where(
        lane < half, pltpu.roll(tile, TILE - half, 1), pltpu.roll(tile, half, 1)
    )
    return tile * cos_rows + partner * sin_rows


def write_bias(bias, doc_keys, doc_queries):
    seq = bias.shape[0]
    step = 128

    def body(i, carry):
        rows = rows_of(i, step, step)
        keys = doc_keys[rows, :][:, :1]
        same = keys == doc_queries[:1, :]
        spot = lax.broadcasted_iota(jnp.int32, (step, seq), 0) + i * step
        own = spot == lax.broadcasted_iota(jnp.int32, (step, seq), 1)
        bias[rows, :] = jnp.where(jnp.logical_or(same, own), 0.0, masked_score)
        return carry

    lax.fori_loop(0, seq // step, body, 0)


class Gather:
    def __init__(self, ref, layer, sems, first_sem, size, where):
        me, mate, across, far, core = where
        self.across, self.mate = [], []
        self.forward = []
        half = size // 2

        def piece(block, part):
            start = pl.multiple_of(block * size + part * half, half)
            return ref.at[layer, pl.ds(start, half)]

        for part in range(2):
            own = piece(me, part)
            theirs = piece(across, part)
            self.across.append(push(own, own, sems, layer, first_sem + part, across))
            self.mate.append(push(own, own, sems, layer, first_sem + 2 + part, mate))
            self.forward.append(push(theirs, theirs, sems, layer, first_sem + 4 + part, mate))

    def start(self):
        for copy in self.across + self.mate:
            copy.start()

    def wait_mate(self):
        for copy in self.mate:
            copy.wait_recv()

    def wait_across(self):
        for copy, onward in zip(self.across, self.forward):
            copy.wait_recv()
            onward.start()

    def wait_far(self):
        for copy in self.forward:
            copy.wait_recv()

    def finish(self):
        for copy in self.across + self.mate + self.forward:
            copy.wait_send()


class Scatter:
    def __init__(self, part, slot, got, layer, sems, first_sem, where):
        me, mate, across, far, core = where
        self.part, self.slot, self.got, self.layer = part, slot, got, layer
        self.far = push(part.at[slot, 0], got.at[layer, 0], sems, layer, first_sem, mate)
        self.over = push(part.at[slot, 1], got.at[layer, 1], sems, layer, first_sem + 1, across)
        self.near = push(part.at[slot, 2], got.at[layer, 2], sems, layer, first_sem + 2, mate)

    def send_far(self, block):
        self.part[self.slot, 0] = block.astype(bf16)
        self.far.start()

    def send_across(self, block):
        self.far.wait_recv()
        self.part[self.slot, 1] = (block + self.got[self.layer, 0].astype(f32)).astype(bf16)
        self.over.start()

    def send_mate(self, block):
        self.part[self.slot, 2] = block.astype(bf16)
        self.near.start()

    def total(self, block):
        self.near.wait_recv()
        self.over.wait_recv()
        return (
            block
            + self.got[self.layer, 1].astype(f32)
            + self.got[self.layer, 2].astype(f32)
        )

    def finish(self):
        for copy in (self.far, self.over, self.near):
            copy.wait_send()


def normed_rows(rows):
    centered = rows - jnp.mean(rows, axis=-1, keepdims=True)
    inverse = lax.rsqrt(jnp.mean(centered * centered, axis=-1, keepdims=True) + norm_epsilon)
    return centered * inverse, inverse


def forward_kernel(
    tok, wq_in, wo_in, wg_in, wd_in, gain, cos_rows, sin_rows, doc_keys, doc_queries,
    act_out, xf_out, qkv_out, lse_out, att_out, flow_out, gu_out, hid_out,
    n1_out, s1_out, n2_out, s2_out,
    wq, wo, wg, wd, xf, qkv, att, flow, gu, hid, bias, vt, k2, lse,
    n1, s1, n2, s2, first, act, part, got, sems, wsems, osems,
):
    where = places()
    me, mate, across, far, core = where
    size = tok.shape[0]
    seq = size * GROUP
    ff = hid.shape[2]
    weights = []
    for layer in range(LAYERS):
        for number, (source, target) in enumerate(((wq_in, wq), (wo_in, wo), (wg_in, wg), (wd_in, wd))):
            copy = pltpu.make_async_copy(source.at[layer], target.at[layer], wsems.at[layer, number])
            copy.start()
            weights.append(copy)
    xf[0, rows_of(me, size, size), :] = tok[...]
    greet(mate, across)
    pending = []
    stores = []

    def store(number, layer, source, target):
        copy = pltpu.make_async_copy(source.at[layer], target.at[layer], osems.at[layer, number])
        copy.start()
        stores.append(copy)

    row_gather = Gather(xf, 0, sems, 0, size, where)
    row_gather.start()
    write_bias(bias, doc_keys, doc_queries)
    low_mask, high_mask = half_masks()

    for layer in range(LAYERS):
        weights[4 * layer].wait()

        def project(block, layer=layer):
            rows = rows_of(block, size, size)
            proj = dot(xf[layer, rows, :], wq[layer])
            c, s = cos_rows[rows, :], sin_rows[rows, :]
            for tile in (0, 1, 3):
                piece = proj[:, tile * TILE:(tile + 1) * TILE]
                qkv[layer, rows, tile * TILE:(tile + 1) * TILE] = turn(piece, c, s).astype(bf16)
            for tile in (2, 4):
                piece = proj[:, tile * TILE:(tile + 1) * TILE]
                qkv[layer, rows, tile * TILE:(tile + 1) * TILE] = piece.astype(bf16)

        project(me)
        row_gather.wait_mate()
        project(mate)
        row_gather.wait_across()
        project(across)
        row_gather.wait_far()
        project(far)
        pending.append(row_gather)
        store(0, layer, xf, xf_out)
        store(1, layer, qkv, qkv_out)
        vt[0] = qkv[layer, :, 2 * TILE:3 * TILE].T
        vt[1] = qkv[layer, :, 4 * TILE:5 * TILE].T
        k2[...] = pltpu.roll(qkv[layer, :, 3 * TILE:4 * TILE].astype(f32), HEAD_DIM, 1).astype(bf16)

        sends = []
        forwards = []
        for head in range(OWN_HEADS):
            query_tile = (0, 0, 3)[head]
            mask = (low_mask, high_mask, low_mask)[head]

            def attend(i, carry, layer=layer, head=head, query_tile=query_tile, mask=mask):
                rows = rows_of(i, size, size)
                queries = qkv[layer, rows, query_tile * TILE:(query_tile + 1) * TILE] * mask
                keys = k2[...] if head == 2 else qkv[layer, :, TILE:2 * TILE]
                values = (vt.at[0, :HEAD_DIM], vt.at[0, HEAD_DIM:], vt.at[1, HEAD_DIM:])[head][...]
                scores = dot_nt(keys, queries) * (score_scale * log2e) + bias[:, rows]
                top = jnp.max(scores, axis=0, keepdims=True)
                probs = jnp.exp2(scores - top)
                total = jnp.sum(probs, axis=0, keepdims=True)
                result = dot(values, probs.astype(bf16)) / total
                spot = pl.ds(
                    pl.multiple_of(me * (OWN_HEADS * HEAD_DIM) + head * HEAD_DIM, HEAD_DIM), HEAD_DIM
                )
                att[layer, spot, rows] = result.astype(bf16)
                lse[layer, head:head + 1, rows] = top + jnp.log(total) * log2e
                return carry

            lax.fori_loop(0, seq // size, attend, 0)

            def features(block, head=head, layer=layer):
                start = block * (OWN_HEADS * HEAD_DIM) + head * HEAD_DIM
                return att.at[layer, pl.ds(pl.multiple_of(start, HEAD_DIM), HEAD_DIM)]

            own, theirs = features(me), features(across)
            to_across = push(own, own, sems, layer, 6 + head, across)
            to_mate = push(own, own, sems, layer, 9 + head, mate)
            onward = push(theirs, theirs, sems, layer, 12 + head, mate)
            to_across.start()
            to_mate.start()
            if head:
                sends[-2].wait_recv()
                forwards[-1].start()
            sends += [to_across, to_mate]
            forwards.append(onward)
        sends[-2].wait_recv()
        forwards[-1].start()
        for head in range(OWN_HEADS):
            sends[2 * head + 1].wait_recv()
            forwards[head].wait_recv()
        store(2, layer, lse, lse_out)
        store(3, layer, att, att_out)
        for number in range(1, 4):
            weights[4 * layer + number].wait()

        def feed(block, keep, layer=layer):
            rows = rows_of(block, size, size)
            branch = dot_tn(att[layer, :, rows], wo[layer])
            normed, inverse = normed_rows(xf[layer, rows, :].astype(f32) + branch)
            first_rows = normed * gain[layer, 0:1, :]
            if keep:
                n1[layer] = normed
                s1[layer] = jnp.broadcast_to(inverse, s1.shape[1:])
                first[...] = first_rows
            first_low = first_rows.astype(bf16)
            flow[layer, rows, :] = first_low
            gate_up = dot(first_low, wg[layer])
            gate, upward = gate_up[:, :ff], gate_up[:, ff:]
            gu[layer, rows, :] = gate_up.astype(bf16)
            hidden = (gate / (1.0 + jnp.exp(-gate)) * upward).astype(bf16)
            hid[layer, rows, :] = hidden
            return dot_nt(hidden, wd[layer])

        scatter = Scatter(part, layer, got, layer, sems, 15, where)
        scatter.send_far(feed(far, False))
        scatter.send_across(feed(across, False))
        scatter.send_mate(feed(mate, False))
        own_part = feed(me, True)
        store(4, layer, flow, flow_out)
        store(5, layer, gu, gu_out)
        store(6, layer, hid, hid_out)
        store(7, layer, n1, n1_out)
        store(8, layer, s1, s1_out)
        ffn = scatter.total(own_part)
        pending.append(scatter)
        normed, inverse = normed_rows(first[...] + ffn)
        n2[layer] = normed
        s2[layer] = jnp.broadcast_to(inverse, s2.shape[1:])
        result = (normed * gain[layer, 1:2, :]).astype(bf16)
        store(9, layer, n2, n2_out)
        store(10, layer, s2, s2_out)
        if layer + 1 < LAYERS:
            xf[layer + 1, rows_of(me, size, size), :] = result
            row_gather = Gather(xf, layer + 1, sems, 0, size, where)
            row_gather.start()
        else:
            act[...] = result
            copy = pltpu.make_async_copy(act, act_out, osems.at[0, 11])
            copy.start()
            stores.append(copy)
        for copy in sends + forwards:
            copy.wait_send()
    for item in pending:
        item.finish()
    for copy in stores:
        copy.wait()


def backward_kernel(
    cot, n1_in, s1_in, n2_in, s2_in, xf_in, qkv_in, lse_in, att_in, flow_in, gu_in, hid_in,
    wq_in, wo_in, wg_in, wd_in, gain, cos_rows, sin_rows, doc_keys, doc_queries,
    ig_out, gq_out, go_out, gg_out, gd_out, gain_out,
    n1, s1, n2, s2, xf, qkv, lse, att, flow, gu, hid, wq, wo, wg, wd,
    bias, dff, dbr, dgu, datt, dproj, dk, dv, dqt, kt, k2, grad, part, got,
    gq, go, gg, gd, sems, lsems, osems,
):
    where = places()
    me, mate, across, far, core = where
    size = cot.shape[0]
    seq = size * GROUP
    ff = hid.shape[1]
    feats = xf.shape[1]
    own_feats = OWN_HEADS * HEAD_DIM
    held = dict(
        n2=(n2_in, n2), s2=(s2_in, s2), wd=(wd_in, wd), gu=(gu_in, gu), wg=(wg_in, wg),
        hid=(hid_in, hid), n1=(n1_in, n1), s1=(s1_in, s1), flow=(flow_in, flow), wo=(wo_in, wo),
        qkv=(qkv_in, qkv), lse=(lse_in, lse), att=(att_in, att), wq=(wq_in, wq), xf=(xf_in, xf),
    )
    order = list(held)
    loads = {}

    def load(name, layer):
        if layer < 0:
            return
        source, target = held[name]
        copy = pltpu.make_async_copy(source.at[layer], target, lsems.at[order.index(name)])
        copy.start()
        loads[name] = copy

    for name in order:
        load(name, LAYERS - 1)
    greet(mate, across)
    write_bias(bias, doc_keys, doc_queries)
    low_mask, high_mask = half_masks()
    grad[...] = cot[...]
    pending = []
    scatters = []
    stores = {}

    def store(number, layer, source, target):
        copy = pltpu.make_async_copy(source, target.at[layer], osems.at[layer, number])
        copy.start()
        stores[number] = copy

    def stored(number):
        if number in stores:
            stores.pop(number).wait()

    for layer in range(LAYERS - 1, -1, -1):

        def norm_back(grad_rows, normed, inverse, row, layer=layer):
            gain_out[layer, row:row + 1, :] = jnp.sum(grad_rows * normed, axis=0, keepdims=True)
            scaled = grad_rows * gain[layer, row:row + 1, :]
            return (
                scaled
                - jnp.mean(scaled, axis=-1, keepdims=True)
                - normed * jnp.mean(scaled * normed, axis=-1, keepdims=True)
            ) * inverse

        loads["n2"].wait()
        loads["s2"].wait()
        dz = norm_back(grad[...], n2[...], s2[:, :1], 1)
        load("n2", layer - 1)
        load("s2", layer - 1)
        grad[...] = dz
        dff[layer, rows_of(me, size, size), :] = dz.astype(bf16)
        gather = Gather(dff, layer, sems, 0, size, where)
        gather.start()
        for name in ("wd", "gu", "wg"):
            loads[name].wait()

        def feed_back(block, layer=layer):
            rows = rows_of(block, size, size)
            grad_hidden = dot(dff[layer, rows, :], wd[...])
            gate = gu[rows, :ff].astype(f32)
            upward = gu[rows, ff:].astype(f32)
            sigma = 1.0 / (1.0 + jnp.exp(-gate))
            up_grad = grad_hidden * gate * sigma
            gate_grad = grad_hidden * upward * sigma * (1.0 + gate * (1.0 - sigma))
            dgu[rows, :ff] = gate_grad.astype(bf16)
            dgu[rows, ff:] = up_grad.astype(bf16)
            return dot_nt(dgu[rows, :], wg[...])

        if len(scatters) > 1:
            scatters[-2].finish()
        scatter = Scatter(part, 0, got, 2 * layer, sems, 6, where)
        scatters.append(scatter)
        own_part = feed_back(me)
        gather.wait_mate()
        scatter.send_mate(feed_back(mate))
        gather.wait_across()
        across_part = feed_back(across)
        gather.wait_far()
        scatter.send_far(feed_back(far))
        pending.append(gather)
        scatter.send_across(across_part)
        load("gu", layer - 1)
        load("wd", layer - 1)
        load("wg", layer - 1)
        loads["hid"].wait()

        stored(3)

        def down_weight(i, carry, layer=layer):
            cols = rows_of(i, 256, 256)
            gd[cols, :] = dot_tn(dff[layer, :, cols], hid[...]).astype(bf16)
            return carry

        lax.fori_loop(0, feats // 256, down_weight, 0)
        store(3, layer, gd, gd_out)
        load("hid", layer - 1)

        dfirst = grad[...] + scatter.total(own_part)
        loads["n1"].wait()
        loads["s1"].wait()
        dr = norm_back(dfirst, n1[...], s1[:, :1], 0)
        load("n1", layer - 1)
        load("s1", layer - 1)
        grad[...] = dr
        dbr[layer, rows_of(me, size, size), :] = dr.astype(bf16)
        gather = Gather(dbr, layer, sems, 9, size, where)
        gather.start()
        loads["flow"].wait()

        stored(2)

        def gate_up_weight(i, carry, layer=layer):
            cols = rows_of(i, 256, 256)
            gg[cols, :] = dot_tn(flow[:, cols], dgu[...]).astype(bf16)
            return carry

        lax.fori_loop(0, feats // 256, gate_up_weight, 0)
        store(2, layer, gg, gg_out)
        load("flow", layer - 1)

        loads["wo"].wait()

        def att_back(block, layer=layer):
            rows = rows_of(block, size, size)
            for tile, start in enumerate((0, HEAD_DIM)):
                spot = pl.ds(pl.multiple_of(me * own_feats + start, HEAD_DIM), TILE)
                datt[rows, tile * TILE:(tile + 1) * TILE] = dot_nt(
                    dbr[layer, rows, :], wo[spot, :]
                ).astype(bf16)

        att_back(me)
        gather.wait_mate()
        att_back(mate)
        gather.wait_across()
        att_back(across)
        gather.wait_far()
        att_back(far)
        pending.append(gather)
        load("wo", layer - 1)

        loads["qkv"].wait()
        loads["lse"].wait()
        kt[0] = qkv[:, TILE:2 * TILE].T
        kt[1] = qkv[:, 3 * TILE:4 * TILE].T
        k2[...] = pltpu.roll(qkv[:, 3 * TILE:4 * TILE].astype(f32), HEAD_DIM, 1).astype(bf16)
        dk[...] = jnp.zeros_like(dk)
        dv[...] = jnp.zeros_like(dv)
        for head in range(OWN_HEADS):
            tile = head // 2
            query_tile = (0, 0, 3)[head]
            value_tile = (2, 2, 4)[head]
            query_mask = (low_mask, high_mask, low_mask)[head]
            value_mask = (low_mask, high_mask, high_mask)[head]

            def attend(i, carry, head=head, tile=tile, query_tile=query_tile, value_tile=value_tile,
                       query_mask=query_mask, value_mask=value_mask):
                rows = rows_of(i, size, size)
                queries = qkv[rows, query_tile * TILE:(query_tile + 1) * TILE] * query_mask
                keys = k2[...] if head == 2 else qkv[:, TILE:2 * TILE]
                scores = dot_nt(keys, queries) * (score_scale * log2e) + bias[:, rows]
                probs = jnp.exp2(scores - lse[head:head + 1, rows])
                outs = datt[rows, tile * TILE:(tile + 1) * TILE] * value_mask
                grad_probs = dot_nt(qkv[:, value_tile * TILE:(value_tile + 1) * TILE], outs)
                delta = jnp.sum(probs * grad_probs, axis=0, keepdims=True)
                grad_scores = (probs * (grad_probs - delta)).astype(bf16)
                dv[tile] = dv[tile] + dot(probs.astype(bf16), outs)
                dk[tile] = dk[tile] + dot(grad_scores, queries)
                keys_t = (kt.at[0, :HEAD_DIM], kt.at[0, HEAD_DIM:], kt.at[1, HEAD_DIM:])[head][...]
                spot = (0, HEAD_DIM, 0)[head]
                dqt[tile, spot:spot + HEAD_DIM, rows] = dot(keys_t, grad_scores)
                return carry

            lax.fori_loop(0, seq // size, attend, 0)

        def unrotate(i, carry):
            rows = rows_of(i, size, size)
            c, s = cos_rows[rows, :], -sin_rows[rows, :]
            dproj[rows, :TILE] = turn(dqt[0, :, rows].T * score_scale, c, s).astype(bf16)
            dproj[rows, TILE:2 * TILE] = turn(dk[0, rows, :] * score_scale, c, s).astype(bf16)
            dproj[rows, 2 * TILE:3 * TILE] = dv[0, rows, :].astype(bf16)
            lower = lane_iota((size, TILE)) < HEAD_DIM
            mixed = jnp.where(lower, dqt[1, :, rows].T, pltpu.roll(dk[1, rows, :], HEAD_DIM, 1))
            dproj[rows, 3 * TILE:4 * TILE] = turn(mixed * score_scale, c, s).astype(bf16)
            dproj[rows, 4 * TILE:] = dv[1, rows, :].astype(bf16)
            return carry

        lax.fori_loop(0, seq // size, unrotate, 0)
        load("qkv", layer - 1)
        load("lse", layer - 1)
        loads["wq"].wait()

        def input_part(block):
            return dot_nt(dproj[rows_of(block, size, size), :], wq[...])

        if len(scatters) > 1:
            scatters[-2].finish()
        scatter = Scatter(part, 1, got, 2 * layer + 1, sems, 6, where)
        scatters.append(scatter)
        scatter.send_far(input_part(far))
        scatter.send_across(input_part(across))
        scatter.send_mate(input_part(mate))
        own_part = input_part(me)
        load("wq", layer - 1)
        loads["xf"].wait()

        stored(0)

        def qkv_weight(i, carry, layer=layer):
            cols = rows_of(i, 256, 256)
            gq[cols, :] = dot_tn(xf[:, cols], dproj[...]).astype(bf16)
            return carry

        lax.fori_loop(0, feats // 256, qkv_weight, 0)
        store(0, layer, gq, gq_out)
        load("xf", layer - 1)
        loads["att"].wait()

        stored(1)

        def out_weight(i, carry, layer=layer):
            rows = rows_of(i, 256, 256)
            half = feats // 2
            cols = pl.ds(pl.multiple_of(core * half, half), half)
            go[rows, :] = dot(att[rows, :], dbr[layer, :, cols]).astype(bf16)
            return carry

        lax.fori_loop(0, feats // 256, out_weight, 0)
        store(1, layer, go, go_out)
        load("att", layer - 1)
        grad[...] = grad[...] + scatter.total(own_part)
    copy = pltpu.make_async_copy(grad, ig_out, osems.at[0, 4])
    copy.start()
    copy.wait()
    for item in pending + scatters[-2:]:
        item.finish()
    for number in range(4):
        stored(number)


def pack_documents(length_row, mask_row):
    seq = mask_row.shape[0]
    ends = jnp.cumsum(length_row)
    spots = jnp.arange(seq, dtype=jnp.int32)
    past = spots[:, None] >= ends[None, :]
    number = jnp.sum(past.astype(jnp.int32), axis=1)
    starts = jnp.max(jnp.where(past, ends[None, :], 0), axis=1)
    position = spots - starts
    keys = jnp.where(mask_row == 1, number, -1)
    doc_keys = jnp.broadcast_to(keys[:, None], (seq, 128))
    doc_queries = jnp.broadcast_to(number[None, :], (8, seq))
    half = HEAD_DIM // 2
    freq = jnp.power(rotary_base, -2.0 * jnp.arange(half).astype(f32) / HEAD_DIM)
    angle = position.astype(f32)[:, None] * freq
    c, s = jnp.cos(angle), jnp.sin(angle)
    cos_rows = jnp.concatenate([c, c, c, c], axis=1)
    sin_rows = jnp.concatenate([-s, s, -s, s], axis=1)
    return cos_rows, sin_rows, doc_keys, doc_queries


def own_projection(weight, me):
    layers, rows, _ = weight.shape
    split = weight.reshape(layers, rows, 3, HEADS * HEAD_DIM)
    own = lax.dynamic_slice_in_dim(split, me * OWN_HEADS * HEAD_DIM, OWN_HEADS * HEAD_DIM, 3)
    own = own.astype(bf16)
    pairs = own[..., :TILE].reshape(layers, rows, 3 * TILE)
    last = own[..., TILE:]
    return jnp.concatenate(
        [pairs, last[:, :, 0], last[:, :, 1], jnp.zeros_like(last[:, :, 0]), last[:, :, 2]], axis=-1
    )


def whole_projection(grad):
    group, layers, rows, _ = grad.shape
    pairs = grad[..., :3 * TILE].reshape(group, layers, rows, 3, TILE)
    last = jnp.stack(
        [
            grad[..., 3 * TILE:3 * TILE + HEAD_DIM],
            grad[..., 3 * TILE + HEAD_DIM:4 * TILE],
            grad[..., 4 * TILE + HEAD_DIM:],
        ],
        axis=3,
    )
    full = jnp.concatenate([pairs, last], axis=-1)
    return full.transpose(1, 2, 3, 0, 4).reshape(layers, rows, 3 * HEADS * HEAD_DIM)


def run_forward(tokens, weights, gain, tables):
    size, feats = tokens.shape
    seq = size * GROUP
    ff = weights[3].shape[2]
    shapes = dict(
        act=((size, feats), bf16),
        xf=((LAYERS, seq, feats), bf16),
        qkv=((LAYERS, seq, PROJ), bf16),
        lse=((LAYERS, 8, seq), f32),
        att=((LAYERS, feats, seq), bf16),
        flow=((LAYERS, seq, feats), bf16),
        gu=((LAYERS, seq, 2 * ff), bf16),
        hid=((LAYERS, seq, ff), bf16),
        n1=((LAYERS, size, feats), f32),
        s1=((LAYERS, size, 128), f32),
        n2=((LAYERS, size, feats), f32),
        s2=((LAYERS, size, 128), f32),
    )
    held = {name: pltpu.VMEM(*shape) for name, shape in shapes.items()}
    scratch = [pltpu.VMEM(w.shape, bf16) for w in weights]
    scratch += [held[n] for n in ("xf", "qkv", "att", "flow", "gu", "hid")]
    scratch += [
        pltpu.VMEM((seq, seq), f32),
        pltpu.VMEM((2, TILE, seq), bf16),
        pltpu.VMEM((seq, TILE), bf16),
        held["lse"],
    ]
    scratch += [held[n] for n in ("n1", "s1", "n2", "s2")]
    scratch += [
        pltpu.VMEM((size, feats), f32),
        held["act"],
        pltpu.VMEM((LAYERS, 3, size, feats), bf16),
        pltpu.VMEM((LAYERS, 3, size, feats), bf16),
        pltpu.SemaphoreType.DMA((2, LAYERS, 18)),
        pltpu.SemaphoreType.DMA((LAYERS, 4)),
        pltpu.SemaphoreType.DMA((LAYERS, 12)),
    ]
    return pl.pallas_call(
        forward_kernel,
        out_shape=[jax.ShapeDtypeStruct(*shape) for shape in shapes.values()],
        in_specs=[VMEM] + [ANY] * 4 + [VMEM] * 5,
        out_specs=[ANY] * len(shapes),
        scratch_shapes=scratch,
        compiler_params=pltpu.CompilerParams(
            collective_id=0, has_side_effects=True, vmem_limit_bytes=VMEM_LIMIT
        ),
        cost_estimate=pl.CostEstimate(
            flops=12 * 10**9, bytes_accessed=60 * 10**6, transcendentals=10**7
        ),
        name="forward",
    )(tokens, *weights, gain, *tables)


def run_backward(cotangent, kept, weights, gain, tables):
    size, feats = cotangent.shape
    seq = size * GROUP
    xf, qkv, lse, att, flow, gu, hid, n1, s1, n2, s2 = kept
    ff = hid.shape[2]
    wq, wo, wg, wd = weights
    loaded = [n1, s1, n2, s2, xf, qkv, lse, att, flow, gu, hid, wq, wo, wg, wd]
    outs = [
        ((size, feats), f32),
        (wq.shape, bf16),
        ((LAYERS, feats, feats // 2), bf16),
        (wg.shape, bf16),
        (wd.shape, bf16),
        ((LAYERS, 2, feats), f32),
    ]
    scratch = [pltpu.VMEM(a.shape[1:], a.dtype) for a in loaded]
    scratch += [
        pltpu.VMEM((seq, seq), f32),
        pltpu.VMEM((LAYERS, seq, feats), bf16),
        pltpu.VMEM((LAYERS, seq, feats), bf16),
        pltpu.VMEM((seq, 2 * ff), bf16),
        pltpu.VMEM((seq, 2 * TILE), bf16),
        pltpu.VMEM((seq, PROJ), bf16),
        pltpu.VMEM((2, seq, TILE), f32),
        pltpu.VMEM((2, seq, TILE), f32),
        pltpu.VMEM((2, TILE, seq), f32),
        pltpu.VMEM((2, TILE, seq), bf16),
        pltpu.VMEM((seq, TILE), bf16),
        pltpu.VMEM((size, feats), f32),
        pltpu.VMEM((2, 3, size, feats), bf16),
        pltpu.VMEM((2 * LAYERS, 3, size, feats), bf16),
    ]
    scratch += [pltpu.VMEM(shape[1:], kind) for shape, kind in outs[1:5]]
    scratch += [
        pltpu.SemaphoreType.DMA((2, 2 * LAYERS, 15)),
        pltpu.SemaphoreType.DMA((len(loaded),)),
        pltpu.SemaphoreType.DMA((LAYERS, 5)),
    ]
    return pl.pallas_call(
        backward_kernel,
        out_shape=[jax.ShapeDtypeStruct(*shape) for shape in outs],
        in_specs=[VMEM] + [ANY] * 15 + [VMEM] * 5,
        out_specs=[ANY] * 5 + [VMEM],
        scratch_shapes=scratch,
        compiler_params=pltpu.CompilerParams(
            collective_id=1, has_side_effects=True, vmem_limit_bytes=VMEM_LIMIT
        ),
        cost_estimate=pl.CostEstimate(
            flops=24 * 10**9, bytes_accessed=60 * 10**6, transcendentals=10**7
        ),
        name="backward",
    )(cotangent, *loaded, gain, *tables)


def adamw(weight, first, second, average, gradient, rate, decay):
    first_new = beta_first * first + (1.0 - beta_first) * gradient
    second_new = beta_second * second + (1.0 - beta_second) * gradient * gradient
    first_hat = first_new / (1.0 - beta_first**STEP)
    second_hat = second_new / (1.0 - beta_second**STEP)
    weight_new = weight - rate * (
        first_hat / (jnp.sqrt(second_hat) + adam_epsilon) + decay * weight
    )
    average_new = average_decay * average + (1.0 - average_decay) * weight_new
    return (gradient, first_new, second_new, weight_new, average_new)


def shards(
    tokens,
    cotangent,
    lengths,
    key_mask,
    qkv_weight,
    qkv_first,
    qkv_second,
    qkv_average,
    out_weight,
    out_first,
    out_second,
    out_average,
    gate_up_weight,
    gate_up_first,
    gate_up_second,
    gate_up_average,
    down_weight,
    down_first,
    down_second,
    down_average,
    norm_gain,
    gain_first,
    gain_second,
    gain_average,
):
    me = lax.axis_index("mp")
    own = gate_up_weight.shape[1]
    ff = gate_up_weight.shape[3]
    gain = lax.all_gather(norm_gain, "dp", axis=2, tiled=True)
    tables = pack_documents(lengths[0], key_mask)
    owned = (
        own_projection(qkv_weight, me),
        out_weight.astype(bf16),
        gate_up_weight.reshape(LAYERS, own, 2 * ff).astype(bf16),
        down_weight.astype(bf16),
    )
    weights = [lax.all_gather(w, "dp", axis=1, tiled=True) for w in owned]
    act, *kept = run_forward(tokens, weights, gain, tables)
    input_grad, gq, go, gg, gd, gain_part = run_backward(cotangent, kept, weights, gain, tables)
    gq, go, gg, gd = [
        lax.psum_scatter(g, "dp", scatter_dimension=1, tiled=True) for g in (gq, go, gg, gd)
    ]
    qkv_grad = whole_projection(lax.all_gather(gq, "mp").astype(f32))
    go = lax.all_gather(go, "mp")
    out_grad = jnp.concatenate([go[0], go[1]], axis=-1).astype(f32)
    gate_up_grad = gg.reshape(LAYERS, own, 2, ff).astype(f32)
    down_grad = gd.astype(f32)
    gain_grad = lax.psum_scatter(
        lax.psum(gain_part, "mp"), "dp", scatter_dimension=2, tiled=True
    )
    results = [act, input_grad]
    results.extend(adamw(qkv_weight, qkv_first, qkv_second, qkv_average, qkv_grad, 0.03, 0.01))
    results.extend(adamw(out_weight, out_first, out_second, out_average, out_grad, 0.5, 0.01))
    results.extend(
        adamw(
            gate_up_weight, gate_up_first, gate_up_second, gate_up_average, gate_up_grad, 0.03, 0.01
        )
    )
    results.extend(
        adamw(down_weight, down_first, down_second, down_average, down_grad, 0.02, 0.01)
    )
    results.extend(adamw(norm_gain, gain_first, gain_second, gain_average, gain_grad, 0.6, 0.0))
    return tuple(results)


def solution(mesh):
    return jax.shard_map(
        shards,
        mesh=mesh,
        in_specs=(
            P(("dp", "mp"), None),
            P(("dp", "mp"), None),
            P("dp", None),
            P("dp"),
            P(None, "dp", None),
            P(None, "dp", None),
            P(None, "dp", None),
            P(None, "dp", None),
            P(None, "dp", None),
            P(None, "dp", None),
            P(None, "dp", None),
            P(None, "dp", None),
            P(None, "dp", None, "mp"),
            P(None, "dp", None, "mp"),
            P(None, "dp", None, "mp"),
            P(None, "dp", None, "mp"),
            P(None, "dp", "mp"),
            P(None, "dp", "mp"),
            P(None, "dp", "mp"),
            P(None, "dp", "mp"),
            P(None, None, "dp"),
            P(None, None, "dp"),
            P(None, None, "dp"),
            P(None, None, "dp"),
        ),
        out_specs=(
            P(("dp", "mp"), None),
            P(("dp", "mp"), None),
            P(None, "dp", None),
            P(None, "dp", None),
            P(None, "dp", None),
            P(None, "dp", None),
            P(None, "dp", None),
            P(None, "dp", None),
            P(None, "dp", None),
            P(None, "dp", None),
            P(None, "dp", None),
            P(None, "dp", None),
            P(None, "dp", None, "mp"),
            P(None, "dp", None, "mp"),
            P(None, "dp", None, "mp"),
            P(None, "dp", None, "mp"),
            P(None, "dp", None, "mp"),
            P(None, "dp", "mp"),
            P(None, "dp", "mp"),
            P(None, "dp", "mp"),
            P(None, "dp", "mp"),
            P(None, "dp", "mp"),
            P(None, None, "dp"),
            P(None, None, "dp"),
            P(None, None, "dp"),
            P(None, None, "dp"),
            P(None, None, "dp"),
        ),
        check_vma=False,
    )
```

time: 1750 us -> 878 us (0.50)
  matrix products: 550 us -> 0 us
  waiting for transfers between devices: 839 us -> 518 us
  Pallas kernels: 0 us -> 230 us
  local copies, waits for them, and re-layouts: 169 us -> 22.3 us
  other arithmetic: 105 us -> 28 us
  blocking collectives: 40.5 us -> 58 us
    dot_general x191 -> x0, matrix products: 542 us -> none  [the longest x48 147 us: one_head(): lax.dot_general(head_query, head_keys, (((1,), (1,)), ((), ())), preferre...]
    reduce_scatter x12 -> x4, waiting for transfers between devices: 664 us -> 259 us  [shards(): lax.psum_scatter(g, 'dp', scatter_dimension=1, tiled=True)]
    pallas_call x0 -> x2, Pallas kernels: none -> 230 us  [the longest x1 137 us: run_backward(): pl.pallas_call(backward_kernel, out_shape=[jax.ShapeDtypeStruct(*shape) f...]
    unnamed x170 -> x54, local copies, waits for them, and re-layouts: 74.4 us -> 5.26 us
    unnamed x28 -> x10, waiting for transfers between devices: 2.97 us -> 59 us
    while x48 -> x0, local copies, waits for them, and re-layouts: 47.7 us -> none
    convert_element_type x32 -> x4, other arithmetic: 38.8 us -> 1.9 us  [the longest x1 0.74 us: shards(): out_weight.astype(bf16)]
    all_gather x14 -> x4, waiting for transfers between devices: 172 us -> 200 us  [shards(): weights = [lax.all_gather(w, 'dp', axis=1, tiled=True) for w in owned]]
  transfers between devices with their start and end apart: 27 -> 9, of which waited for: 16 -> 9; matrix products, arithmetic and copies ran while one was open for 31% -> 4% of each run, Pallas kernels for 0% -> 0%
where the time goes in v1:
time: 878 us; the launch traced here: 871 us
  waiting for transfers between devices  518 us (59%)
  Pallas kernels  230 us (26%)
  blocking collectives  58 us (7%)
  other arithmetic  28 us (3%)
  local copies, waits for them, and re-layouts  22.3 us (3%)
  between operations  14.7 us (2%)
    reduce_scatter x4, waiting for transfers between devices, shards(): lax.psum_scatter(g, 'dp', scatter_dimension=1, tiled=True)  259 us
    all_gather x4, waiting for transfers between devices, shards(): weights = [lax.all_gather(w, 'dp', axis=1, tiled=True) for w in owned]  200 us
    pallas_call x1, Pallas kernels, run_backward(): pl.pallas_call(backward_kernel, out_shape=[jax.ShapeDtypeStruct(*shape) f...  137 us
    pallas_call x1, Pallas kernels, run_forward(): pl.pallas_call(forward_kernel, out_shape=[jax.ShapeDtypeStruct(*shape) fo...  93 us
    unnamed x10, waiting for transfers between devices  59 us
    all_gather x1, blocking collectives, shards(): gain = lax.all_gather(norm_gain, 'dp', axis=2, tiled=True)  34.8 us
    add x5, other arithmetic, adamw(): average_new = average_decay * average + (1.0 - average_decay) * weight_new  20.4 us
  transfers between devices with their start and end apart: 9, of which 9 were waited for; matrix products, arithmetic and copies ran while one was open for 4% of the time, Pallas kernels for 0%

profile of v1, /device:TPU:0, one launch (start us, length us, event | category | flops | bytes accessed | tf_op | source)
XLA Modules:
  0.0 871.1 jit_solution(14553433623146326041)
XLA Ops:
  7.3 2.4 reshape.110
  13.2 1.2 convert_element_type.50
  14.6 34.8 %all_gather.31 = f32[2,2,768]{1,0,2:T(2,128)S(1)} all-gather(f32[2,2,96]{1,0,2:T(2,128)S(1)} %copy.80), channel_id=1, replica_groups=mesh['dp'=8,'mp'=4] {'dp'}, dimensions={2}, use_global_device_ids=true | all-gather | bytes 13824 | tf_op jit(solution)/shard_map/all_gather | solution.py:809
  50.6 1.9 fusion.4
  52.5 1.8 pad_maximum_fusion
  54.4 10.8 %all-gather.7.cloned.1.call-done.wq_in = bf16[2,768,640]{2,1,0:T(8,128)(2,1)} async-done(((bf16[2,96,640]{2,1,0:T(8,128)(2,1)}), bf16[2,768,640]{2,1,0:T(8,128)(2,1)}) %all-gather.7.cloned.1.call-update) | async-done | bytes 1966096 | tf_op jit(solution)/shard_map/all_gather | solution.py:817
  65.2 54.4 %all-gather.9.cloned.1.call-done.wo_in = bf16[2,768,768]{2,1,0:T(8,128)(2,1)} async-done(((bf16[2,96,768]{2,1,0:T(8,128)(2,1)}), bf16[2,768,768]{2,1,0:T(8,128)(2,1)}) %all-gather.9.cloned.1.call-update) | async-done | bytes 2359312 | tf_op jit(solution)/shard_map/all_gather | solution.py:817
  119.6 53.3 %all-gather.13.cloned.1.call-done.wd_in = bf16[2,768,768]{2,1,0:T(8,128)(2,1)} async-done(((bf16[2,96,768]{2,1,0:T(8,128)(2,1)}), bf16[2,768,768]{2,1,0:T(8,128)(2,1)}) %all-gather.13.cloned.1.call-update) | async-done | bytes 2359312 | tf_op jit(solution)/shard_map/all_gather | solution.py:817
  172.9 81.1 %all-gather.11.cloned.1.call-done.wg_in = bf16[2,768,1536]{2,1,0:T(8,128)(2,1)} async-done(((bf16[2,96,1536]{2,1,0:T(8,128)(2,1)}), bf16[2,768,1536]{2,1,0:T(8,128)(2,1)}) %all-gather.11.cloned.1.call-update) | async-done | bytes 4718608 | tf_op jit(solution)/shard_map/all_gather | solution.py:817
  254.0 1.0 broadcast_in_dim.23.doc_keys
  255.6 93.0 %forward.1 = (bf16[256,768]{1,0:T(8,128)(2,1)}, bf16[2,1024,768]{2,1,0:T(8,128)(2,1)}, bf16[2,1024,640]{2,1,0:T(8,128)(2,1)}, f32[2,8,1024]{2,1,0:T(8,128)}, bf1...) custom-call(bf16[256,768]{1,0:T(8,128)(2,1)} %tok.1, ...), custom_call_target="tpu_custom_call" | custom-call | flops 12000000000 | bytes 60000000 | tf_op jit(solution)/shard_map/forward/pallas_call | solution.py:698
  348.6 137.0 %backward.1 = (f32[256,768]{1,0:T(8,128)}, bf16[2,768,640]{2,1,0:T(8,128)(2,1)}, bf16[2,768,384]{2,1,0:T(8,128)(2,1)}, bf16[2,768,1536]{2,1,0:T(8,128)(2,1)}, bf...) custom-call(f32[256,768]{1,0:T(8,128)} %cot.1, f32[2,256,768]{2,1,0:T(8,128)} %get-tuple-element.46.n1_in, ...), custom_call_target="tpu_custom_call" | custom-call | flops 24000000000 | bytes 60000000 | tf_op jit(solution)/shard_map/backward/pallas_call | solution.py:752
  485.6 1.2 copy.87
  486.8 1.2 reshape.124
  490.8 56.4 %reduce-scatter.16.cloned.1.call-done = f32[96,4]{1,0:T(8,128)} async-done(((f32[768,4]{1,0:T(8,128)}), f32[96,4]{1,0:T(8,128)}) %reduce-scatter.16.cloned.1.call-update) | async-done | bytes 1552
  548.2 5.6 psum.8
  554.5 59.0 %reduce-scatter.10.cloned.1.call-done = bf16[2,96,384]{2,1,0:T(8,128)(2,1)} async-done(((bf16[2,768,384]{2,1,0:T(8,128)(2,1)}), bf16[2,96,384]{2,1,0:T(8,128)(2,1)}) %reduce-scatter.10.cloned.1.call-update) | async-done | bytes 147472 | tf_op jit(solution)/shard_map/reduce_scatter | solution.py:821
  613.5 7.7 all-gather.1
  621.3 1.8 add_multiply_fusion.3
  623.1 59.7 %reduce-scatter.8.cloned.1.call-done = bf16[2,96,640]{2,1,0:T(8,128)(2,1)} async-done(((bf16[2,768,640]{2,1,0:T(8,128)(2,1)}), bf16[2,96,640]{2,1,0:T(8,128)(2,1)}) %reduce-scatter.8.cloned.1.call-update) | async-done | bytes 245776 | tf_op jit(solution)/shard_map/reduce_scatter | solution.py:821
  682.8 9.9 %all-gather = bf16[8,96,640]{2,1,0:T(8,128)(2,1)S(1)} all-gather(bf16[2,96,640]{2,1,0:T(8,128)(2,1)} %reduce-scatter.8.cloned.1.call-done), channel_id=2, replica_groups=mesh['dp'=8,'mp'=4] {'mp'}, dimensions={0}, use_global_device_ids=true | all-gather | bytes 1228800 | tf_op jit(solution)/shard_map/all_gather | solution.py:823
  692.7 1.1 slice.50
  693.8 2.1 reshape.114
  696.1 1.7 maximum_bitcast_fusion
  697.8 1.5 copy.86
  699.3 2.8 reshape.115
  702.1 7.8 add_multiply_fusion
  709.9 44.8 %reduce-scatter.14.cloned.1.call-done = bf16[2,96,768]{2,1,0:T(8,128)(2,1)} async-done(((bf16[2,768,768]{2,1,0:T(8,128)(2,1)}), bf16[2,96,768]{2,1,0:T(8,128)(2,1)}) %reduce-scatter.14.cloned.1.call-update) | async-done | bytes 294928 | tf_op jit(solution)/shard_map/reduce_scatter | solution.py:821
  754.7 2.8 add_multiply_fusion.2
  757.5 95.6 %reduce-scatter.12.cloned.1.call-done = bf16[2,96,1536]{2,1,0:T(8,128)(2,1)} async-done(((bf16[2,768,1536]{2,1,0:T(8,128)(2,1)}), bf16[2,96,1536]{2,1,0:T(8,128)(2,1)}) %reduce-scatter.12.cloned.1.call-update) | async-done | bytes 589840 | tf_op jit(solution)/shard_map/reduce_scatter | solution.py:821
  853.1 2.0 reshape.116
  855.1 7.3 add_multiply_fusion.1
  (88 shorter events, 11.7 us)
Async XLA Ops:
  7.2 58.0 %all-gather.7.cloned.1.call-start = ((), (), s32[]{:S(2)}) async-start(), calls=%async_computation.5 | async-start | bytes 2211840 | tf_op jit(solution)/shard_map/all_gather | solution.py:817
  9.7 1.4 copy-start.3
  10.0 1.9 copy-start.5
  10.1 2.6 copy-start
  11.0 108.6 %all-gather.9.cloned.1.call-start = ((), (), s32[]{:S(2)}) async-start(), calls=%async_computation.6 | async-start | bytes 2654208 | tf_op jit(solution)/shard_map/all_gather | solution.py:817
  11.8 161.1 %all-gather.13.cloned.1.call-start = ((), (), s32[]{:S(2)}) async-start(), calls=%async_computation.8 | async-start | bytes 2654208 | tf_op jit(solution)/shard_map/all_gather | solution.py:817
  12.7 1.8 copy-start.16
  12.7 241.3 %all-gather.11.cloned.1.call-start = ((), (), s32[]{:S(2)}) async-start(), calls=%async_computation.7 | async-start | bytes 5308416 | tf_op jit(solution)/shard_map/all_gather | solution.py:817
  13.1 37.2 %copy-start.22 = (s32[1,8]{1,0:T(1,128)S(1)}, s32[1,8]{1,0:T(1,128)}, u32[]{:S(2)}) copy-start(s32[1,8]{1,0:T(1,128)} %param.26) | copy-start | bytes 100
  14.4 532.8 %reduce-scatter.16.cloned.1.call-start = ((), (), s32[]{:S(2)}) async-start(), calls=%async_computation.13 | async-start | bytes 442368
  50.6 3.8 copy-start.18
  488.0 125.5 %reduce-scatter.10.cloned.1.call-start = ((), (), s32[]{:S(2)}) async-start(), calls=%async_computation.10 | async-start | bytes 1327104 | tf_op jit(solution)/shard_map/reduce_scatter | solution.py:821
  488.6 194.2 %reduce-scatter.8.cloned.1.call-start = ((), (), s32[]{:S(2)}) async-start(), calls=%async_computation.9 | async-start | bytes 2211840 | tf_op jit(solution)/shard_map/reduce_scatter | solution.py:821
  489.3 265.4 %reduce-scatter.14.cloned.1.call-start = ((), (), s32[]{:S(2)}) async-start(), calls=%async_computation.12 | async-start | bytes 2654208 | tf_op jit(solution)/shard_map/reduce_scatter | solution.py:821
  490.1 363.0 %reduce-scatter.12.cloned.1.call-start = ((), (), s32[]{:S(2)}) async-start(), calls=%async_computation.11 | async-start | bytes 5308416 | tf_op jit(solution)/shard_map/reduce_scatter | solution.py:821
  490.1 63.7 %copy-start.19 = (f32[2,2,96]{2,1,0:T(2,128)S(1)}, f32[2,2,96]{2,1,0:T(2,128)}, u32[]{:S(2)}) copy-start(f32[2,2,96]{2,1,0:T(2,128)} %param.47) | copy-start | bytes 4612
  490.1 63.7 %copy-start.20 = (f32[2,2,96]{2,1,0:T(2,128)S(1)}, f32[2,2,96]{2,1,0:T(2,128)}, u32[]{:S(2)}) copy-start(f32[2,2,96]{2,1,0:T(2,128)} %param.46) | copy-start | bytes 4612
  490.1 63.7 %copy-start.21 = (f32[2,2,96]{2,1,0:T(2,128)S(1)}, f32[2,2,96]{2,1,0:T(2,128)}, u32[]{:S(2)}) copy-start(f32[2,2,96]{2,1,0:T(2,128)} %param.45) | copy-start | bytes 4612
  490.2 131.1 %copy-start.10 = (f32[2,96,768]{2,1,0:T(8,128)S(1)}, f32[2,96,768]{2,1,0:T(8,128)}, u32[]{:S(2)}) copy-start(f32[2,96,768]{2,1,0:T(8,128)} %param.34) | copy-start | bytes 1769476
  490.2 131.1 %copy-start.11 = (f32[2,96,768]{2,1,0:T(8,128)S(1)}, f32[2,96,768]{2,1,0:T(8,128)}, u32[]{:S(2)}) copy-start(f32[2,96,768]{2,1,0:T(8,128)} %param.33) | copy-start | bytes 1769476
  490.8 130.5 %copy-start.4 = (f32[2,96,768]{2,1,0:T(8,128)S(1)}, f32[2,96,768]{2,1,0:T(8,128)}, u32[]{:S(2)}) copy-start(f32[2,96,768]{2,1,0:T(8,128)} %param.32) | copy-start | bytes 1769476
  490.8 130.5 %copy-start.9 = (f32[2,96,768]{2,1,0:T(8,128)S(1)}, f32[2,96,768]{2,1,0:T(8,128)}, u32[]{:S(2)}) copy-start(f32[2,96,768]{2,1,0:T(8,128)} %param.35) | copy-start | bytes 1769476
  553.9 69.2 %copy-start.17 = (f32[2,2,96]{2,1,0:T(2,128)}, f32[2,2,96]{2,1,0:T(2,128)S(1)}, u32[]{:S(2)}) copy-start(f32[2,2,96]{2,1,0:T(2,128)S(1)} %psum.8) | copy-start | bytes 4612
  702.0 52.6 %copy-start.6 = (f32[2,96,768]{2,1,0:T(8,128)S(1)}, f32[2,96,768]{2,1,0:T(8,128)}, u32[]{:S(2)}) copy-start(f32[2,96,768]{2,1,0:T(8,128)} %param.40) | copy-start | bytes 1769476
  702.1 52.6 %copy-start.12 = (f32[2,96,768]{2,1,0:T(8,128)S(1)}, f32[2,96,768]{2,1,0:T(8,128)}, u32[]{:S(2)}) copy-start(f32[2,96,768]{2,1,0:T(8,128)} %param.43) | copy-start | bytes 1769476
  702.1 52.6 %copy-start.13 = (f32[2,96,768]{2,1,0:T(8,128)S(1)}, f32[2,96,768]{2,1,0:T(8,128)}, u32[]{:S(2)}) copy-start(f32[2,96,768]{2,1,0:T(8,128)} %param.42) | copy-start | bytes 1769476
  702.1 52.6 %copy-start.14 = (f32[2,96,768]{2,1,0:T(8,128)S(1)}, f32[2,96,768]{2,1,0:T(8,128)}, u32[]{:S(2)}) copy-start(f32[2,96,768]{2,1,0:T(8,128)} %param.41) | copy-start | bytes 1769476
  754.7 100.4 %copy-start.7 = (f32[2,96,2,768]{3,2,1,0:T(2,128)S(1)}, f32[2,96,2,768]{3,2,1,0:T(2,128)}, u32[]{:S(2)}) copy-start(f32[2,96,2,768]{3,2,1,0:T(2,128)} %param.39) | copy-start | bytes 3538948
  757.5 97.5 %copy-start.1 = (f32[2,96,2,768]{3,2,1,0:T(2,128)S(1)}, f32[2,96,2,768]{3,2,1,0:T(2,128)}, u32[]{:S(2)}) copy-start(f32[2,96,2,768]{3,2,1,0:T(2,128)} %param.36) | copy-start | bytes 3538948
  855.1 7.4 copy-start.2
  855.1 7.4 copy-start.15
  855.1 8.1 copy-start.8
Sparse Core Ops, SparseCore 0:
  11.1 54.0 all-gather.6
  68.0 51.6 all-gather.8
  122.4 50.4 all-gather.12
  175.5 78.4 all-gather.10
  488.1 59.0 reduce-scatter.15
  550.5 63.0 reduce-scatter.9
  617.0 65.7 reduce-scatter.7
  686.7 67.9 reduce-scatter.13
  758.8 94.2 reduce-scatter.11

commit v2 on v1

--- a/solution.py
+++ b/solution.py
@@ -13,6 +13,7 @@
 LAYERS = 2
 STEP = 10
 GROUP = 4
+DEPTH = 4
 OWN_HEADS = HEADS // GROUP
 TILE = 2 * HEAD_DIM
 PROJ = 5 * TILE
@@ -65,11 +66,214 @@
     )
 
 
-def greet(mate, across):
+class Spread:
+    def __init__(self, own):
+        index = lax.axis_index("dp")
+        self.own = own
+        self.z, self.x = lax.div(index, 2), lax.rem(index, 2)
+
+    def device(self, step):
+        return 2 * lax.rem(self.z + step, DEPTH) + self.x
+
+    def beside(self, step):
+        return 2 * lax.rem(self.z + step, DEPTH) + 1 - self.x
+
+    def rows(self, index):
+        return pl.ds(pl.multiple_of(index * self.own, self.own), self.own)
+
+
+def greet(mate, across, far=None, spread=None):
     barrier = pltpu.get_barrier_semaphore()
-    for who in (mate, across):
+    packs = [mate, across] if far is None else [mate, across, far]
+    for who in packs:
         pl.semaphore_signal(barrier, inc=1, device_id={"mp": who}, device_id_type=MESH)
-    pl.semaphore_wait(barrier, 2)
+    others = []
+    if spread is not None:
+        others = [spread.beside(0)] + [spread.device(step) for step in range(1, DEPTH)]
+        for who in others:
+            pl.semaphore_signal(barrier, inc=1, device_id={"dp": who}, device_id_type=MESH)
+    pl.semaphore_wait(barrier, len(packs) + len(others))
+
+
+def ship(src, dst, sems, piece, number, who):
+    return pltpu.make_async_remote_copy(
+        src_ref=src,
+        dst_ref=dst,
+        send_sem=sems.at[0, piece, number],
+        recv_sem=sems.at[1, piece, number],
+        device_id={"dp": who},
+        device_id_type=MESH,
+    )
+
+
+class WeightGather:
+    def __init__(self, source, target, layer, piece, sems, local, spread, cols=None):
+        self.target, self.layer, self.cols = target, layer, cols
+        self.piece, self.sems, self.spread = piece, sems, spread
+        z, x = spread.z, spread.x
+        own = source.at[layer] if cols is None else source.at[layer, :, cols]
+        place = self.view(z, x)
+        self.local = pltpu.make_async_copy(
+            source.at[layer], target.at[layer, spread.rows(2 * z + x)], local
+        )
+        self.beside = self.send(own, place, 0, 0, 2 * z + 1 - x)
+        self.up = self.send(own, place, 1, 1 + z, 2 * jnp.minimum(z + 1, DEPTH - 1) + x)
+        self.down = self.send(own, place, 2, 1 + z, 2 * jnp.maximum(z - 1, 0) + x)
+        self.hops = [(far, way) for far in range(1, DEPTH) for way in (-1, 1)]
+        self.todo = list(self.hops)
+
+    def view(self, z, x):
+        rows = self.spread.rows(2 * z + x)
+        if self.cols is None:
+            return self.target.at[self.layer, rows]
+        return self.target.at[self.layer, rows, self.cols]
+
+    def send(self, src, dst, out, into, who):
+        return pltpu.make_async_remote_copy(
+            src_ref=src,
+            dst_ref=dst,
+            send_sem=self.sems.at[0, self.piece, out],
+            recv_sem=self.sems.at[1, self.piece, into],
+            device_id={"dp": who},
+            device_id_type=MESH,
+        )
+
+    def start(self):
+        self.local.start()
+        pl.when(self.spread.z < DEPTH - 1)(self.up.start)
+        pl.when(self.spread.z > 0)(self.down.start)
+        self.beside.start()
+
+    def hop(self, far, way):
+        z, x = self.spread.z, self.spread.x
+        source = jnp.clip(z + way * far, 0, DEPTH - 1)
+        block = self.view(source, x)
+        onward = jnp.clip(z - way, 0, DEPTH - 1)
+        arrive = self.send(block, block, 3 + source, 1 + source, 2 * source + x)
+        over = self.send(block, block, 3 + source, 1 + DEPTH + source, 2 * z + 1 - x)
+        along = self.send(block, block, 3 + DEPTH + source, 1 + source, 2 * onward + x)
+        comes = z >= far if way < 0 else z + far < DEPTH
+        goes = z > 0 if way > 0 else z < DEPTH - 1
+        return arrive, over, along, comes, jnp.logical_and(comes, goes)
+
+    def serve(self, count=2 * DEPTH):
+        while self.todo and count:
+            count -= 1
+            arrive, over, along, comes, goes = self.hop(*self.todo.pop(0))
+
+            def receive():
+                arrive.wait_recv()
+                over.start()
+
+            pl.when(comes)(receive)
+            pl.when(goes)(along.start)
+
+    def wait(self):
+        self.serve()
+        self.local.wait()
+        self.beside.wait_recv()
+        z, x = self.spread.z, self.spread.x
+        for step in range(1, DEPTH):
+            source = lax.rem(z + step, DEPTH)
+            block = self.view(source, 1 - x)
+            self.send(block, block, 3, 1 + DEPTH + source, 2 * z + 1 - x).wait_recv()
+
+    def finish(self):
+        self.beside.wait_send()
+        pl.when(self.spread.z < DEPTH - 1)(self.up.wait_send)
+        pl.when(self.spread.z > 0)(self.down.wait_send)
+        for far, way in self.hops:
+            arrive, over, along, comes, goes = self.hop(far, way)
+            pl.when(comes)(over.wait_send)
+            pl.when(goes)(along.wait_send)
+
+
+class HalfGather(WeightGather):
+    def __init__(self, source, target, layer, piece, sems, local, spread, half, pack_sems, where):
+        me, mate, across, far, core = where
+        cols = pl.ds(pl.multiple_of(core * half, half), half)
+        super().__init__(source, target, layer, piece, sems, local, spread, cols)
+        self.swap = []
+        for step in range(DEPTH):
+            z = lax.rem(spread.z + step, DEPTH)
+            for number, x in enumerate((spread.x, 1 - spread.x)):
+                if step or number:
+                    block = self.view(z, x)
+                    self.swap.append(
+                        push(block, block, pack_sems, layer, 2 * step + number - 1, mate)
+                    )
+
+    def share(self):
+        super().wait()
+        for copy in self.swap:
+            copy.start()
+
+    def wait(self):
+        for copy in self.swap:
+            copy.wait_recv()
+
+    def finish(self):
+        super().finish()
+        for copy in self.swap:
+            copy.wait_send()
+
+
+class WeightSum:
+    def __init__(self, grad, near, apart, piece, sems, spread, credits, again, more, total):
+        self.grad, self.near, self.apart, self.spread = grad, near, apart, spread
+        self.near_credit, self.apart_credit = credits
+        self.again, self.more = again, more
+        self.sum = total
+        self.beside = [
+            ship(grad.at[spread.rows(spread.beside(step))], near.at[step], sems, piece, step,
+                 spread.beside(0))
+            for step in range(DEPTH)
+        ]
+        self.along = [
+            ship(grad.at[spread.rows(spread.device(step))], apart.at[step - 1], sems, piece,
+                 DEPTH - 1 + step, spread.device(step))
+            for step in range(1, DEPTH)
+        ]
+
+    def start(self):
+        if self.again:
+            pl.semaphore_wait(self.near_credit, 1)
+        for copy in self.beside[1:] + self.beside[:1]:
+            copy.start()
+
+    def credit(self, sem, who):
+        pl.semaphore_signal(sem, inc=1, device_id={"dp": who}, device_id_type=MESH)
+
+    def add(self):
+        if self.again:
+            pl.semaphore_wait(self.apart_credit, DEPTH - 1)
+        for step in range(1, DEPTH):
+            self.beside[step].wait_recv()
+            rows = self.spread.rows(self.spread.device(step))
+            self.grad[rows, :] = (
+                self.grad[rows, :].astype(f32) + self.near[step].astype(f32)
+            ).astype(bf16)
+            self.along[step - 1].start()
+        self.beside[0].wait_recv()
+        rows = self.spread.rows(self.spread.device(0))
+        self.sum[...] = self.grad[rows, :].astype(f32) + self.near[0].astype(f32)
+        if self.more:
+            self.credit(self.near_credit, self.spread.beside(0))
+
+    def total(self):
+        for copy in self.along:
+            copy.wait_recv()
+        result = self.sum[...]
+        for step in range(DEPTH - 1):
+            result = result + self.apart[step].astype(f32)
+        if self.more:
+            for step in range(1, DEPTH):
+                self.credit(self.apart_credit, self.spread.device(step))
+        return result
+
+    def finish(self):
+        for copy in self.beside + self.along:
+            copy.wait_send()
 
 
 def rows_of(block, size, extent):
@@ -111,7 +315,7 @@
 
 
 class Gather:
-    def __init__(self, ref, layer, sems, first_sem, size, where):
+    def __init__(self, ref, slot, layer, sems, first_sem, size, where):
         me, mate, across, far, core = where
         self.across, self.mate = [], []
         self.forward = []
@@ -119,7 +323,7 @@
 
         def piece(block, part):
             start = pl.multiple_of(block * size + part * half, half)
-            return ref.at[layer, pl.ds(start, half)]
+            return ref.at[slot, pl.ds(start, half)]
 
         for part in range(2):
             own = piece(me, part)
@@ -150,13 +354,38 @@
             copy.wait_send()
 
 
+class Share:
+    def __init__(self, ref, layer, sems, first_sem, where):
+        me, mate, across, far, core = where
+        own, theirs = ref.at[layer, me], ref.at[layer, across]
+        self.ref, self.layer, self.me = ref, layer, me
+        self.over = push(own, own, sems, layer, first_sem, across)
+        self.near = push(own, own, sems, layer, first_sem + 1, mate)
+        self.onward = push(theirs, theirs, sems, layer, first_sem + 2, mate)
+
+    def start(self, block):
+        self.ref[self.layer, self.me] = block
+        self.over.start()
+        self.near.start()
+
+    def serve(self):
+        self.over.wait_recv()
+        self.onward.start()
+
+    def finish(self):
+        self.near.wait_recv()
+        self.onward.wait_recv()
+        for copy in (self.over, self.near, self.onward):
+            copy.wait_send()
+
+
 class Scatter:
     def __init__(self, part, slot, got, layer, sems, first_sem, where):
         me, mate, across, far, core = where
-        self.part, self.slot, self.got, self.layer = part, slot, got, layer
-        self.far = push(part.at[slot, 0], got.at[layer, 0], sems, layer, first_sem, mate)
-        self.over = push(part.at[slot, 1], got.at[layer, 1], sems, layer, first_sem + 1, across)
-        self.near = push(part.at[slot, 2], got.at[layer, 2], sems, layer, first_sem + 2, mate)
+        self.part, self.slot, self.got = part, slot, got
+        self.far = push(part.at[slot, 0], got.at[slot, 0], sems, layer, first_sem, mate)
+        self.over = push(part.at[slot, 1], got.at[slot, 1], sems, layer, first_sem + 1, across)
+        self.near = push(part.at[slot, 2], got.at[slot, 2], sems, layer, first_sem + 2, mate)
 
     def send_far(self, block):
         self.part[self.slot, 0] = block.astype(bf16)
@@ -164,7 +393,7 @@
 
     def send_across(self, block):
         self.far.wait_recv()
-        self.part[self.slot, 1] = (block + self.got[self.layer, 0].astype(f32)).astype(bf16)
+        self.part[self.slot, 1] = (block + self.got[self.slot, 0].astype(f32)).astype(bf16)
         self.over.start()
 
     def send_mate(self, block):
@@ -176,8 +405,8 @@
         self.over.wait_recv()
         return (
             block
-            + self.got[self.layer, 1].astype(f32)
-            + self.got[self.layer, 2].astype(f32)
+            + self.got[self.slot, 1].astype(f32)
+            + self.got[self.slot, 2].astype(f32)
         )
 
     def finish(self):
@@ -192,25 +421,71 @@
 
 
 def forward_kernel(
-    tok, wq_in, wo_in, wg_in, wd_in, gain, cos_rows, sin_rows, doc_keys, doc_queries,
+    spreading, tok, wq_in, wo_in, wg_in, wd_in, gain_in, cos_rows, sin_rows, doc_keys, doc_queries,
     act_out, xf_out, qkv_out, lse_out, att_out, flow_out, gu_out, hid_out,
-    n1_out, s1_out, n2_out, s2_out,
+    n1_out, s1_out, n2_out, s2_out, wq_out, wo_out, wg_out, wd_out, gain,
     wq, wo, wg, wd, xf, qkv, att, flow, gu, hid, bias, vt, k2, lse,
-    n1, s1, n2, s2, first, act, part, got, sems, wsems, osems,
+    n1, s1, n2, s2, first, act, part, got, sems, wsems, osems, dsems, ssems, gside, gdeep, gsems,
 ):
     where = places()
     me, mate, across, far, core = where
+    weight_outs = (wq_out, wo_out, wg_out, wd_out)
     size = tok.shape[0]
     seq = size * GROUP
     ff = hid.shape[2]
+    spread = Spread(wq_in.shape[1]) if spreading else None
     weights = []
     for layer in range(LAYERS):
         for number, (source, target) in enumerate(((wq_in, wq), (wo_in, wo), (wg_in, wg), (wd_in, wd))):
-            copy = pltpu.make_async_copy(source.at[layer], target.at[layer], wsems.at[layer, number])
-            copy.start()
-            weights.append(copy)
+            local = wsems.at[layer, number]
+            if not spreading:
+                weights.append(pltpu.make_async_copy(source.at[layer], target.at[layer], local))
+            elif number == 1:
+                weights.append(
+                    HalfGather(source, target, layer, 4 * layer + 1, dsems, local, spread,
+                               wo.shape[2] // 2, ssems, where)
+                )
+            else:
+                weights.append(
+                    WeightGather(source, target, layer, 4 * layer + number, dsems, local, spread)
+                )
     xf[0, rows_of(me, size, size), :] = tok[...]
-    greet(mate, across)
+    greet(mate, across, None, spread)
+    gains = []
+    if spreading:
+        gdeep[spread.z] = gain_in[...]
+        own = gdeep.at[spread.z]
+        for step in range(1, DEPTH):
+            gains.append(ship(own, own, gsems, 0, step, spread.device(step)))
+            gains[-1].start()
+    else:
+        gain[...] = gain_in[...]
+    for item in weights:
+        item.start()
+
+    def gain_stage(stage):
+        if not spreading:
+            return
+        if stage == 0:
+            for copy in gains:
+                copy.wait_recv()
+            gside[spread.x] = gdeep[0] + gdeep[1] + gdeep[2] + gdeep[3]
+            own = gside.at[spread.x]
+            gains.append(ship(own, own, gsems, 0, 0, spread.beside(0)))
+            gains[-1].start()
+        else:
+            gains[-1].wait_recv()
+            gain[...] = gside[0] + gside[1]
+            for copy in gains:
+                copy.wait_send()
+
+    def serve(layer, number, count=2 * DEPTH):
+        if spreading and layer < LAYERS:
+            item = weights[4 * layer + number]
+            if number == 1:
+                item.share()
+            else:
+                item.serve(count)
     pending = []
     stores = []
 
@@ -219,13 +494,16 @@
         copy.start()
         stores.append(copy)
 
-    row_gather = Gather(xf, 0, sems, 0, size, where)
+    row_gather = Gather(xf, 0, 0, sems, 0, size, where)
     row_gather.start()
     write_bias(bias, doc_keys, doc_queries)
     low_mask, high_mask = half_masks()
 
     for layer in range(LAYERS):
         weights[4 * layer].wait()
+        serve(layer, 1)
+        if layer == 0:
+            gain_stage(0)
 
         def project(block, layer=layer):
             rows = rows_of(block, size, size)
@@ -290,6 +568,7 @@
             if head:
                 sends[-2].wait_recv()
                 forwards[-1].start()
+            serve(layer, 2, 2)
             sends += [to_across, to_mate]
             forwards.append(onward)
         sends[-2].wait_recv()
@@ -299,6 +578,9 @@
             forwards[head].wait_recv()
         store(2, layer, lse, lse_out)
         store(3, layer, att, att_out)
+        serve(layer, 3)
+        if layer == 0:
+            gain_stage(1)
         for number in range(1, 4):
             weights[4 * layer + number].wait()
 
@@ -306,7 +588,7 @@
             rows = rows_of(block, size, size)
             branch = dot_tn(att[layer, :, rows], wo[layer])
             normed, inverse = normed_rows(xf[layer, rows, :].astype(f32) + branch)
-            first_rows = normed * gain[layer, 0:1, :]
+            first_rows = normed * gain[2 * layer:2 * layer + 1, :]
             if keep:
                 n1[layer] = normed
                 s1[layer] = jnp.broadcast_to(inverse, s1.shape[1:])
@@ -325,6 +607,7 @@
         scatter.send_across(feed(across, False))
         scatter.send_mate(feed(mate, False))
         own_part = feed(me, True)
+        serve(layer + 1, 0)
         store(4, layer, flow, flow_out)
         store(5, layer, gu, gu_out)
         store(6, layer, hid, hid_out)
@@ -335,12 +618,12 @@
         normed, inverse = normed_rows(first[...] + ffn)
         n2[layer] = normed
         s2[layer] = jnp.broadcast_to(inverse, s2.shape[1:])
-        result = (normed * gain[layer, 1:2, :]).astype(bf16)
+        result = (normed * gain[2 * layer + 1:2 * layer + 2, :]).astype(bf16)
         store(9, layer, n2, n2_out)
         store(10, layer, s2, s2_out)
         if layer + 1 < LAYERS:
             xf[layer + 1, rows_of(me, size, size), :] = result
-            row_gather = Gather(xf, layer + 1, sems, 0, size, where)
+            row_gather = Gather(xf, layer + 1, layer + 1, sems, 0, size, where)
             row_gather.start()
         else:
             act[...] = result
@@ -349,20 +632,45 @@
             stores.append(copy)
         for copy in sends + forwards:
             copy.wait_send()
+        if spreading:
+            for number, held in enumerate((wq, wo, wg, wd)):
+                store(12 + number, layer, held, weight_outs[number])
+    if spreading:
+        pending += weights
     for item in pending:
         item.finish()
     for copy in stores:
         copy.wait()
 
 
-def backward_kernel(
-    cot, n1_in, s1_in, n2_in, s2_in, xf_in, qkv_in, lse_in, att_in, flow_in, gu_in, hid_in,
-    wq_in, wo_in, wg_in, wd_in, gain, cos_rows, sin_rows, doc_keys, doc_queries,
-    ig_out, gq_out, go_out, gg_out, gd_out, gain_out,
-    n1, s1, n2, s2, xf, qkv, lse, att, flow, gu, hid, wq, wo, wg, wd,
-    bias, dff, dbr, dgu, datt, dproj, dk, dv, dqt, kt, k2, grad, part, got,
-    gq, go, gg, gd, sems, lsems, osems,
-):
+BACK_LOADED = (
+    "n1", "s1", "n2", "s2", "xf", "qkv", "lse", "att", "flow", "gu", "hid", "wq", "wo", "wg", "wd",
+)
+BACK_TABLES = ("gain", "cos_rows", "sin_rows", "doc_keys", "doc_queries")
+BACK_SCRATCH = (
+    "bias", "dff", "dbr", "datt", "dproj", "dk", "dv", "dqt", "kt", "k2", "grad", "part", "got",
+    "gq", "go", "gg", "gd", "sems", "lsems", "osems",
+)
+BACK_SPREAD = (
+    "gsum", "gpack", "gside", "gdeep", "gsems", "csems", "qshare", "oshare",
+    "near_d", "near_g", "near_u", "near_q", "near_o",
+    "apart_d", "apart_g", "apart_u", "apart_q", "apart_o",
+    "sum_d", "sum_g", "sum_u", "sum_q", "sum_o", "dsems",
+)
+
+
+def backward_kernel(spreading, names, *refs):
+    r = dict(zip(names, refs))
+    cot = r["cot"]
+    gain, cos_rows, sin_rows, doc_keys, doc_queries = (r[n] for n in BACK_TABLES)
+    (
+        bias, dff, dbr, datt, dproj, dk, dv, dqt, kt, k2, grad, part, got,
+        gq, go, gg, gd, sems, lsems, osems,
+    ) = (r[n] for n in BACK_SCRATCH)
+    n1, s1, n2, s2, qkv, lse, att, gu, hid, wq, wo, wg, wd = (
+        r[n] for n in BACK_LOADED if n not in ("xf", "flow")
+    )
+    xf = flow = r["rows"]
     where = places()
     me, mate, across, far, core = where
     size = cot.shape[0]
@@ -370,11 +678,7 @@
     ff = hid.shape[1]
     feats = xf.shape[1]
     own_feats = OWN_HEADS * HEAD_DIM
-    held = dict(
-        n2=(n2_in, n2), s2=(s2_in, s2), wd=(wd_in, wd), gu=(gu_in, gu), wg=(wg_in, wg),
-        hid=(hid_in, hid), n1=(n1_in, n1), s1=(s1_in, s1), flow=(flow_in, flow), wo=(wo_in, wo),
-        qkv=(qkv_in, qkv), lse=(lse_in, lse), att=(att_in, att), wq=(wq_in, wq), xf=(xf_in, xf),
-    )
+    held = {n: (r[n + "_in"], r.get(n, r["rows"])) for n in BACK_LOADED}
     order = list(held)
     loads = {}
 
@@ -386,15 +690,104 @@
         copy.start()
         loads[name] = copy
 
-    for name in order:
+    for name in ("n2", "s2", "wd", "gu", "wg", "hid", "n1", "s1", "flow", "wo", "qkv", "lse", "att", "wq"):
         load(name, LAYERS - 1)
-    greet(mate, across)
+    spread = Spread(feats // (2 * DEPTH)) if spreading else None
+    greet(mate, across, far if spreading else None, spread)
     write_bias(bias, doc_keys, doc_queries)
     low_mask, high_mask = half_masks()
     grad[...] = cot[...]
     pending = []
     scatters = []
     stores = {}
+    sums = {}
+    shares = []
+    pieces = dict(
+        d=gd.at[:, :], g=gg.at[:, :ff], u=gg.at[:, ff:], q=gq.at[:, :], o=go.at[:, :]
+    )
+    gsum = r["gsum"] if spreading else r["gain_out"]
+    gsum[...] = jnp.zeros_like(gsum)
+
+    def begin(name, layer):
+        if not spreading:
+            if name == "u":
+                store(2, layer, gg, r["g_out"])
+            elif name != "g":
+                number = "qogd".index(name)
+                store(number, layer, (gq, go, gg, gd)[number], r[name + "_out"])
+            return
+        index = "dguqo".index(name)
+        item = WeightSum(
+            pieces[name], r["near_" + name], r["apart_" + name], 5 * layer + index, r["dsems"],
+            spread, (r["csems"].at[0, index], r["csems"].at[1, index]),
+            layer < LAYERS - 1, layer > 0, r["sum_" + name],
+        )
+        item.start()
+        sums[name, layer] = item
+
+    def add(name, layer):
+        if spreading and (name, layer) in sums:
+            sums[name, layer].add()
+
+    def total(name, layer):
+        if not spreading or (name, layer) not in sums:
+            return
+        result = sums[name, layer].total()
+        if name == "q":
+            share = Share(r["qshare"], layer, sems, 15, where)
+            share.start(result.astype(bf16))
+            shares.append(share)
+        elif name == "o":
+            oshare = r["oshare"]
+            oshare[layer, core] = result.astype(bf16)
+            copy = push(oshare.at[layer, core], oshare.at[layer, core], sems, layer, 18, mate)
+            copy.start()
+            oshares.append(copy)
+        elif name == "d":
+            r["d_res"][layer] = result
+        else:
+            half = "gu".index(name)
+            r["g_res"][layer, :, half * ff:(half + 1) * ff] = result
+
+    def ready(name, layer):
+        if not spreading:
+            if name != "u":
+                stored("qogd".index(name))
+        elif (name, layer + 1) in sums:
+            sums[name, layer + 1].finish()
+
+    oshares = []
+    gains = []
+
+    def gain_stage(stage):
+        if not spreading:
+            return
+        gpack, gside, gdeep, gsems = (r[n] for n in ("gpack", "gside", "gdeep", "gsems"))
+        if stage == 0:
+            gpack[me] = gsum[...]
+            for number, who in enumerate((mate, across, far)):
+                gains.append(push(gpack.at[me], gpack.at[me], gsems, 0, number, who))
+        elif stage == 1:
+            for copy in gains[:3]:
+                copy.wait_recv()
+            gside[spread.x] = gpack[0] + gpack[1] + gpack[2] + gpack[3]
+            own = gside.at[spread.x]
+            gains.append(ship(own, own, gsems, 0, 3, spread.beside(0)))
+        elif stage == 2:
+            gains[3].wait_recv()
+            gdeep[spread.z] = gside[0] + gside[1]
+            own = gdeep.at[spread.z]
+            for step in range(1, DEPTH):
+                gains.append(ship(own, own, gsems, 0, 3 + step, spread.device(step)))
+        else:
+            for copy in gains[4:]:
+                copy.wait_recv()
+            r["gain_out"][...] = gdeep[0] + gdeep[1] + gdeep[2] + gdeep[3]
+            for copy in gains:
+                copy.wait_send()
+            return
+        for copy in gains[(0, 3, 4)[stage]:]:
+            copy.start()
 
     def store(number, layer, source, target):
         copy = pltpu.make_async_copy(source, target.at[layer], osems.at[layer, number])
@@ -408,8 +801,10 @@
     for layer in range(LAYERS - 1, -1, -1):
 
         def norm_back(grad_rows, normed, inverse, row, layer=layer):
-            gain_out[layer, row:row + 1, :] = jnp.sum(grad_rows * normed, axis=0, keepdims=True)
-            scaled = grad_rows * gain[layer, row:row + 1, :]
+            gsum[2 * layer + row:2 * layer + row + 1, :] = jnp.sum(
+                grad_rows * normed, axis=0, keepdims=True
+            )
+            scaled = grad_rows * gain[2 * layer + row:2 * layer + row + 1, :]
             return (
                 scaled
                 - jnp.mean(scaled, axis=-1, keepdims=True)
@@ -422,23 +817,23 @@
         load("n2", layer - 1)
         load("s2", layer - 1)
         grad[...] = dz
-        dff[layer, rows_of(me, size, size), :] = dz.astype(bf16)
-        gather = Gather(dff, layer, sems, 0, size, where)
+        dff[0, rows_of(me, size, size), :] = dz.astype(bf16)
+        gather = Gather(dff, 0, layer, sems, 0, size, where)
         gather.start()
         for name in ("wd", "gu", "wg"):
             loads[name].wait()
 
         def feed_back(block, layer=layer):
             rows = rows_of(block, size, size)
-            grad_hidden = dot(dff[layer, rows, :], wd[...])
+            grad_hidden = dot(dff[0, rows, :], wd[...])
             gate = gu[rows, :ff].astype(f32)
             upward = gu[rows, ff:].astype(f32)
             sigma = 1.0 / (1.0 + jnp.exp(-gate))
             up_grad = grad_hidden * gate * sigma
             gate_grad = grad_hidden * upward * sigma * (1.0 + gate * (1.0 - sigma))
-            dgu[rows, :ff] = gate_grad.astype(bf16)
-            dgu[rows, ff:] = up_grad.astype(bf16)
-            return dot_nt(dgu[rows, :], wg[...])
+            gu[rows, :ff] = gate_grad.astype(bf16)
+            gu[rows, ff:] = up_grad.astype(bf16)
+            return dot_nt(gu[rows, :], wg[...])
 
         if len(scatters) > 1:
             scatters[-2].finish()
@@ -451,23 +846,23 @@
         across_part = feed_back(across)
         gather.wait_far()
         scatter.send_far(feed_back(far))
-        pending.append(gather)
         scatter.send_across(across_part)
-        load("gu", layer - 1)
         load("wd", layer - 1)
         load("wg", layer - 1)
         loads["hid"].wait()
-
-        stored(3)
+        add("q", layer + 1)
+        ready("d", layer)
 
         def down_weight(i, carry, layer=layer):
             cols = rows_of(i, 256, 256)
-            gd[cols, :] = dot_tn(dff[layer, :, cols], hid[...]).astype(bf16)
+            gd[cols, :] = dot_tn(dff[0, :, cols], hid[...]).astype(bf16)
             return carry
 
         lax.fori_loop(0, feats // 256, down_weight, 0)
-        store(3, layer, gd, gd_out)
+        begin("d", layer)
+        gather.finish()
         load("hid", layer - 1)
+        add("o", layer + 1)
 
         dfirst = grad[...] + scatter.total(own_part)
         loads["n1"].wait()
@@ -477,22 +872,45 @@
         load("s1", layer - 1)
         grad[...] = dr
         dbr[layer, rows_of(me, size, size), :] = dr.astype(bf16)
-        gather = Gather(dbr, layer, sems, 9, size, where)
+        gather = Gather(dbr, layer, layer, sems, 9, size, where)
         gather.start()
         loads["flow"].wait()
 
-        stored(2)
-
-        def gate_up_weight(i, carry, layer=layer):
-            cols = rows_of(i, 256, 256)
-            gg[cols, :] = dot_tn(flow[:, cols], dgu[...]).astype(bf16)
-            return carry
-
-        lax.fori_loop(0, feats // 256, gate_up_weight, 0)
-        store(2, layer, gg, gg_out)
-        load("flow", layer - 1)
+        if layer == 0:
+            gain_stage(0)
+        for name, first_col in (("g", 0), ("u", ff)):
+            ready(name, layer)
+
+            def gate_up_weight(i, carry, first_col=first_col):
+                cols = rows_of(i, 256, 256)
+                gg[cols, first_col:first_col + ff] = dot_tn(
+                    flow[:, cols], gu[:, first_col:first_col + ff]
+                ).astype(bf16)
+                return carry
+
+            lax.fori_loop(0, feats // 256, gate_up_weight, 0)
+            begin(name, layer)
+        load("gu", layer - 1)
+        load("xf", layer)
+        for name in "dgu":
+            total(name, layer + 1)
 
         loads["wo"].wait()
+
+        def weigh_out(layer):
+            loads["att"].wait()
+            ready("o", layer)
+
+            def out_weight(i, carry):
+                rows = rows_of(i, 256, 256)
+                half = feats // 2
+                cols = pl.ds(pl.multiple_of(core * half, half), half)
+                go[rows, :] = dot(att[rows, :], dbr[layer, :, cols]).astype(bf16)
+                return carry
+
+            lax.fori_loop(0, feats // 256, out_weight, 0)
+            begin("o", layer)
+            load("att", layer - 1)
 
         def att_back(block, layer=layer):
             rows = rows_of(block, size, size)
@@ -511,6 +929,12 @@
         att_back(far)
         pending.append(gather)
         load("wo", layer - 1)
+        if layer == 0:
+            weigh_out(layer)
+            gain_stage(1)
+        add("d", layer)
+        total("q", layer + 1)
+        total("o", layer + 1)
 
         loads["qkv"].wait()
         loads["lse"].wait()
@@ -545,6 +969,16 @@
                 return carry
 
             lax.fori_loop(0, seq // size, attend, 0)
+            if head == 0:
+                add("g", layer)
+                for share in shares:
+                    share.serve()
+            if head == 1 and layer == 0:
+                add("o", layer)
+            if layer == 0 and head < 2:
+                gain_stage(2 + head)
+
+        add("u", layer)
 
         def unrotate(i, carry):
             rows = rows_of(i, size, size)
@@ -577,7 +1011,7 @@
         load("wq", layer - 1)
         loads["xf"].wait()
 
-        stored(0)
+        ready("q", layer)
 
         def qkv_weight(i, carry, layer=layer):
             cols = rows_of(i, 256, 256)
@@ -585,30 +1019,35 @@
             return carry
 
         lax.fori_loop(0, feats // 256, qkv_weight, 0)
-        store(0, layer, gq, gq_out)
-        load("xf", layer - 1)
-        loads["att"].wait()
-
-        stored(1)
-
-        def out_weight(i, carry, layer=layer):
-            rows = rows_of(i, 256, 256)
-            half = feats // 2
-            cols = pl.ds(pl.multiple_of(core * half, half), half)
-            go[rows, :] = dot(att[rows, :], dbr[layer, :, cols]).astype(bf16)
-            return carry
-
-        lax.fori_loop(0, feats // 256, out_weight, 0)
-        store(1, layer, go, go_out)
-        load("att", layer - 1)
+        begin("q", layer)
+        load("flow", layer - 1)
+        if layer:
+            weigh_out(layer)
         grad[...] = grad[...] + scatter.total(own_part)
-    copy = pltpu.make_async_copy(grad, ig_out, osems.at[0, 4])
-    copy.start()
-    copy.wait()
+    input_copy = pltpu.make_async_copy(grad, r["ig_out"], osems.at[0, 4])
+    input_copy.start()
+    for name in "dguo":
+        total(name, 0)
+    add("q", 0)
+    total("q", 0)
+    if spreading:
+        shares[-1].serve()
+    input_copy.wait()
     for item in pending + scatters[-2:]:
         item.finish()
     for number in range(4):
         stored(number)
+    for item in shares:
+        item.finish()
+    for copy in oshares:
+        copy.wait()
+    if spreading:
+        for name in "dguqo":
+            sums[name, 0].finish()
+        for number, held in enumerate(((r["qshare"], r["q_out"]), (r["oshare"], r["o_out"]))):
+            copy = pltpu.make_async_copy(*held, osems.at[1, number])
+            copy.start()
+            copy.wait()
 
 
 def pack_documents(length_row, mask_row):
@@ -658,7 +1097,7 @@
     return full.transpose(1, 2, 3, 0, 4).reshape(layers, rows, 3 * HEADS * HEAD_DIM)
 
 
-def run_forward(tokens, weights, gain, tables):
+def run_forward(spreading, tokens, weights, gain, tables):
     size, feats = tokens.shape
     seq = size * GROUP
     ff = weights[3].shape[2]
@@ -675,10 +1114,14 @@
         s1=((LAYERS, size, 128), f32),
         n2=((LAYERS, size, feats), f32),
         s2=((LAYERS, size, 128), f32),
+        wq=((LAYERS, feats, PROJ), bf16),
+        wo=((LAYERS, feats, feats), bf16),
+        wg=((LAYERS, feats, 2 * ff), bf16),
+        wd=((LAYERS, feats, ff), bf16),
+        gain=((8, feats), f32),
     )
     held = {name: pltpu.VMEM(*shape) for name, shape in shapes.items()}
-    scratch = [pltpu.VMEM(w.shape, bf16) for w in weights]
-    scratch += [held[n] for n in ("xf", "qkv", "att", "flow", "gu", "hid")]
+    scratch = [held[n] for n in ("wq", "wo", "wg", "wd", "xf", "qkv", "att", "flow", "gu", "hid")]
     scratch += [
         pltpu.VMEM((seq, seq), f32),
         pltpu.VMEM((2, TILE, seq), bf16),
@@ -693,13 +1136,18 @@
         pltpu.VMEM((LAYERS, 3, size, feats), bf16),
         pltpu.SemaphoreType.DMA((2, LAYERS, 18)),
         pltpu.SemaphoreType.DMA((LAYERS, 4)),
-        pltpu.SemaphoreType.DMA((LAYERS, 12)),
+        pltpu.SemaphoreType.DMA((LAYERS, 16)),
+        pltpu.SemaphoreType.DMA((2, 4 * LAYERS, 3 + 2 * DEPTH)),
+        pltpu.SemaphoreType.DMA((2, LAYERS, 7)),
+        pltpu.VMEM((2, 8, feats), f32),
+        pltpu.VMEM((DEPTH, 8, feats), f32),
+        pltpu.SemaphoreType.DMA((2, 1, DEPTH)),
     ]
     return pl.pallas_call(
-        forward_kernel,
+        functools.partial(forward_kernel, spreading),
         out_shape=[jax.ShapeDtypeStruct(*shape) for shape in shapes.values()],
         in_specs=[VMEM] + [ANY] * 4 + [VMEM] * 5,
-        out_specs=[ANY] * len(shapes),
+        out_specs=[ANY] * (len(shapes) - 1) + [VMEM],
         scratch_shapes=scratch,
         compiler_params=pltpu.CompilerParams(
             collective_id=0, has_side_effects=True, vmem_limit_bytes=VMEM_LIMIT
@@ -711,50 +1159,84 @@
     )(tokens, *weights, gain, *tables)
 
 
-def run_backward(cotangent, kept, weights, gain, tables):
+def run_backward(spreading, cotangent, kept, weights, gain, tables):
     size, feats = cotangent.shape
     seq = size * GROUP
     xf, qkv, lse, att, flow, gu, hid, n1, s1, n2, s2 = kept
     ff = hid.shape[2]
     wq, wo, wg, wd = weights
     loaded = [n1, s1, n2, s2, xf, qkv, lse, att, flow, gu, hid, wq, wo, wg, wd]
-    outs = [
-        ((size, feats), f32),
-        (wq.shape, bf16),
-        ((LAYERS, feats, feats // 2), bf16),
-        (wg.shape, bf16),
-        (wd.shape, bf16),
-        ((LAYERS, 2, feats), f32),
-    ]
-    scratch = [pltpu.VMEM(a.shape[1:], a.dtype) for a in loaded]
-    scratch += [
-        pltpu.VMEM((seq, seq), f32),
-        pltpu.VMEM((LAYERS, seq, feats), bf16),
-        pltpu.VMEM((LAYERS, seq, feats), bf16),
-        pltpu.VMEM((seq, 2 * ff), bf16),
-        pltpu.VMEM((seq, 2 * TILE), bf16),
-        pltpu.VMEM((seq, PROJ), bf16),
-        pltpu.VMEM((2, seq, TILE), f32),
-        pltpu.VMEM((2, seq, TILE), f32),
-        pltpu.VMEM((2, TILE, seq), f32),
-        pltpu.VMEM((2, TILE, seq), bf16),
-        pltpu.VMEM((seq, TILE), bf16),
-        pltpu.VMEM((size, feats), f32),
-        pltpu.VMEM((2, 3, size, feats), bf16),
-        pltpu.VMEM((2 * LAYERS, 3, size, feats), bf16),
-    ]
-    scratch += [pltpu.VMEM(shape[1:], kind) for shape, kind in outs[1:5]]
-    scratch += [
-        pltpu.SemaphoreType.DMA((2, 2 * LAYERS, 15)),
-        pltpu.SemaphoreType.DMA((len(loaded),)),
-        pltpu.SemaphoreType.DMA((LAYERS, 5)),
-    ]
+    own = feats // (2 * DEPTH)
+    half = feats // 2
+    widths = dict(d=ff, g=ff, u=ff, q=PROJ, o=half)
+    if spreading:
+        outs = dict(
+            ig_out=((size, feats), f32),
+            q_out=((LAYERS, GROUP, own, PROJ), bf16),
+            o_out=((LAYERS, 2, own, half), bf16),
+            d_res=((LAYERS, own, ff), f32),
+            g_res=((LAYERS, own, 2 * ff), f32),
+            gain_out=((8, feats), f32),
+        )
+    else:
+        outs = dict(
+            ig_out=((size, feats), f32),
+            q_out=(wq.shape, bf16),
+            o_out=((LAYERS, feats, half), bf16),
+            d_out=(wd.shape, bf16),
+            g_out=(wg.shape, bf16),
+            gain_out=((8, feats), f32),
+        )
+    names = ["cot"] + [n + "_in" for n in BACK_LOADED] + list(BACK_TABLES) + list(outs)
+    scratch = dict(
+        bias=pltpu.VMEM((seq, seq), f32),
+        dff=pltpu.VMEM((1, seq, feats), bf16),
+        dbr=pltpu.VMEM((LAYERS, seq, feats), bf16),
+        datt=pltpu.VMEM((seq, 2 * TILE), bf16),
+        dproj=pltpu.VMEM((seq, PROJ), bf16),
+        dk=pltpu.VMEM((2, seq, TILE), f32),
+        dv=pltpu.VMEM((2, seq, TILE), f32),
+        dqt=pltpu.VMEM((2, TILE, seq), f32),
+        kt=pltpu.VMEM((2, TILE, seq), bf16),
+        k2=pltpu.VMEM((seq, TILE), bf16),
+        grad=pltpu.VMEM((size, feats), f32),
+        part=pltpu.VMEM((2, 3, size, feats), bf16),
+        got=pltpu.VMEM((2, 3, size, feats), bf16),
+        gq=pltpu.VMEM((feats, PROJ), bf16),
+        go=pltpu.VMEM((feats, half), bf16),
+        gg=pltpu.VMEM((feats, 2 * ff), bf16),
+        gd=pltpu.VMEM((feats, ff), bf16),
+        sems=pltpu.SemaphoreType.DMA((2, 2 * LAYERS, 19)),
+        lsems=pltpu.SemaphoreType.DMA((len(loaded),)),
+        osems=pltpu.SemaphoreType.DMA((LAYERS, 5)),
+        rows=pltpu.VMEM((seq, feats), bf16),
+    )
+    for name, array in zip(BACK_LOADED, loaded):
+        if name not in ("xf", "flow"):
+            scratch[name] = pltpu.VMEM(array.shape[1:], array.dtype)
+    if spreading:
+        scratch.update(
+            gsum=pltpu.VMEM((8, feats), f32),
+            gpack=pltpu.VMEM((GROUP, 8, feats), f32),
+            gside=pltpu.VMEM((2, 8, feats), f32),
+            gdeep=pltpu.VMEM((DEPTH, 8, feats), f32),
+            gsems=pltpu.SemaphoreType.DMA((2, 1, 7)),
+            csems=pltpu.SemaphoreType.REGULAR((2, 5)),
+            qshare=pltpu.VMEM((LAYERS, GROUP, own, PROJ), bf16),
+            oshare=pltpu.VMEM((LAYERS, 2, own, half), bf16),
+            dsems=pltpu.SemaphoreType.DMA((2, 5 * LAYERS, 7)),
+        )
+        for name, width in widths.items():
+            scratch["near_" + name] = pltpu.VMEM((DEPTH, own, width), bf16)
+            scratch["apart_" + name] = pltpu.VMEM((DEPTH - 1, own, width), bf16)
+            scratch["sum_" + name] = pltpu.VMEM((own, width), f32)
+    in_vmem = ("d_res", "g_res", "gain_out")
     return pl.pallas_call(
-        backward_kernel,
-        out_shape=[jax.ShapeDtypeStruct(*shape) for shape in outs],
+        functools.partial(backward_kernel, spreading, tuple(names + list(scratch))),
+        out_shape=[jax.ShapeDtypeStruct(*shape) for shape in outs.values()],
         in_specs=[VMEM] + [ANY] * 15 + [VMEM] * 5,
-        out_specs=[ANY] * 5 + [VMEM],
-        scratch_shapes=scratch,
+        out_specs=[VMEM if name in in_vmem else ANY for name in outs],
+        scratch_shapes=list(scratch.values()),
         compiler_params=pltpu.CompilerParams(
             collective_id=1, has_side_effects=True, vmem_limit_bytes=VMEM_LIMIT
         ),
@@ -778,6 +1260,7 @@
 
 
 def shards(
+    spreading,
     tokens,
     cotangent,
     lengths,
@@ -806,7 +1289,15 @@
     me = lax.axis_index("mp")
     own = gate_up_weight.shape[1]
     ff = gate_up_weight.shape[3]
-    gain = lax.all_gather(norm_gain, "dp", axis=2, tiled=True)
+    feats = tokens.shape[1]
+    if spreading:
+        gain = jnp.zeros((8, feats), f32)
+        gain = lax.dynamic_update_slice(
+            gain, norm_gain.reshape(2 * LAYERS, own), (0, lax.axis_index("dp") * own)
+        )
+    else:
+        gain = lax.all_gather(norm_gain, "dp", axis=2, tiled=True).reshape(2 * LAYERS, feats)
+        gain = jnp.concatenate([gain, jnp.zeros((8 - 2 * LAYERS, feats), f32)], axis=0)
     tables = pack_documents(lengths[0], key_mask)
     owned = (
         own_projection(qkv_weight, me),
@@ -814,20 +1305,31 @@
         gate_up_weight.reshape(LAYERS, own, 2 * ff).astype(bf16),
         down_weight.astype(bf16),
     )
-    weights = [lax.all_gather(w, "dp", axis=1, tiled=True) for w in owned]
-    act, *kept = run_forward(tokens, weights, gain, tables)
-    input_grad, gq, go, gg, gd, gain_part = run_backward(cotangent, kept, weights, gain, tables)
-    gq, go, gg, gd = [
-        lax.psum_scatter(g, "dp", scatter_dimension=1, tiled=True) for g in (gq, go, gg, gd)
-    ]
-    qkv_grad = whole_projection(lax.all_gather(gq, "mp").astype(f32))
-    go = lax.all_gather(go, "mp")
+    if not spreading:
+        owned = [lax.all_gather(w, "dp", axis=1, tiled=True) for w in owned]
+    act, *kept = run_forward(spreading, tokens, owned, gain, tables)
+    weights, kept, gain = kept[-5:-1], kept[:-5], kept[-1]
+    backward = run_backward(spreading, cotangent, kept, weights, gain, tables)
+    if spreading:
+        input_grad, gq, go, gd, gg, gain_sum = backward
+        gq, go = gq.transpose(1, 0, 2, 3), go.transpose(1, 0, 2, 3)
+        gain_grad = lax.dynamic_slice_in_dim(
+            gain_sum[:2 * LAYERS].reshape(LAYERS, 2, -1), lax.axis_index("dp") * own, own, 2
+        )
+    else:
+        input_grad, gq, go, gd, gg, gain_sum = backward
+        gq, go, gg, gd = [
+            lax.psum_scatter(g, "dp", scatter_dimension=1, tiled=True) for g in (gq, go, gg, gd)
+        ]
+        gq, go = lax.all_gather(gq, "mp"), lax.all_gather(go, "mp")
+        gain_part = gain_sum[:2 * LAYERS].reshape(LAYERS, 2, -1)
+        gain_grad = lax.psum_scatter(
+            lax.psum(gain_part, "mp"), "dp", scatter_dimension=2, tiled=True
+        )
+    qkv_grad = whole_projection(gq.astype(f32))
     out_grad = jnp.concatenate([go[0], go[1]], axis=-1).astype(f32)
     gate_up_grad = gg.reshape(LAYERS, own, 2, ff).astype(f32)
     down_grad = gd.astype(f32)
-    gain_grad = lax.psum_scatter(
-        lax.psum(gain_part, "mp"), "dp", scatter_dimension=2, tiled=True
-    )
     results = [act, input_grad]
     results.extend(adamw(qkv_weight, qkv_first, qkv_second, qkv_average, qkv_grad, 0.03, 0.01))
     results.extend(adamw(out_weight, out_first, out_second, out_average, out_grad, 0.5, 0.01))
@@ -844,8 +1346,9 @@
 
 
 def solution(mesh):
+    spreading = mesh.shape["dp"] == 2 * DEPTH
     return jax.shard_map(
-        shards,
+        functools.partial(shards, spreading),
         mesh=mesh,
         in_specs=(
             P(("dp", "mp"), None),

time: 878 us -> 424 us (0.48)
  waiting for transfers between devices: 518 us -> 0 us
  Pallas kernels: 230 us -> 361 us
  blocking collectives: 58 us -> 0 us
  between operations: 14.7 us -> 1.48 us
    reduce_scatter x4 -> x0, waiting for transfers between devices: 259 us -> none  [shards(): lax.psum_scatter(g, 'dp', scatter_dimension=1, tiled=True)]
    all_gather x4 -> x0, waiting for transfers between devices: 200 us -> none  [shards(): weights = [lax.all_gather(w, 'dp', axis=1, tiled=True) for w in owned]]
    pallas_call x2, Pallas kernels: 230 us -> 361 us  [the longest x1 187 us: run_backward(): pl.pallas_call(functools.partial(backward_kernel, spreading, tuple(names...]
    unnamed x10 -> x0, waiting for transfers between devices: 59 us -> none
    all_gather x3 -> x0, blocking collectives: 52.4 us -> none  [the longest x1 34.8 us: shards(): gain = lax.all_gather(norm_gain, 'dp', axis=2, tiled=True)]
  transfers between devices with their start and end apart: 9 -> 0, of which waited for: 9 -> 0; matrix products, arithmetic and copies ran while one was open for 4% -> 0% of each run, Pallas kernels for 0% -> 0%
where the time goes in v2:
time: 424 us; the launch traced here: 417 us
  Pallas kernels  361 us (85%)
  other arithmetic  30.1 us (7%)
  local copies, waits for them, and re-layouts  23.7 us (6%)
    pallas_call x1, Pallas kernels, run_backward(): pl.pallas_call(functools.partial(backward_kernel, spreading, tuple(names...  187 us
    pallas_call x1, Pallas kernels, run_forward(): pl.pallas_call(functools.partial(forward_kernel, spreading), out_shape=[j...  174 us
    add x5, other arithmetic, adamw(): average_new = average_decay * average + (1.0 - average_decay) * weight_new  17.9 us

profile of v2, /device:TPU:0, one launch (start us, length us, event | category | flops | bytes accessed | tf_op | source)
XLA Modules:
  0.0 416.6 jit_solution(2640180070976610228)
XLA Ops:
  0.7 0.9 reduce-window.8
  1.7 0.7 subtract_convert_fusion
  2.4 1.5 dynamic_update_slice.3.gain_in
  4.5 1.8 convert_element_type.41.wo_in
  6.4 1.8 convert_element_type.44.wd_in
  8.2 1.0 broadcast_in_dim.41.doc_keys.refs_19_
  9.6 1.2 convert_element_type.43.wg_in
  11.7 0.8 concatenate.15.wq_in
  12.5 1.9 fusion.4
  14.4 1.3 pad_maximum_fusion.2.sin_rows.refs_18_
  15.7 1.3 pad_maximum_fusion.1.cos_rows.refs_17_
  16.9 174.0 %forward.1 = (bf16[256,768]{1,0:T(8,128)(2,1)}, bf16[2,1024,768]{2,1,0:T(8,128)(2,1)}, bf16[2,1024,640]{2,1,0:T(8,128)(2,1)}, f32[2,8,1024]{2,1,0:T(8,128)}, bf1...) custom-call(bf16[256,768]{1,0:T(8,128)(2,1)} %tok.1, ...), custom_call_target="tpu_custom_call" | custom-call | flops 12000000000 | bytes 60000000 | tf_op jit(solution)/shard_map/forward/pallas_call | solution.py:1146
  191.0 187.4 %backward.1 = (f32[256,768]{1,0:T(8,128)}, bf16[2,4,96,640]{3,2,1,0:T(8,128)(2,1)}, bf16[2,2,96,384]{3,2,1,0:T(8,128)(2,1)}, f32[2,96,768]{2,1,0:T(8,128)}, f32[2,96,1536]{2,1,0:T(8,128)}, /*index=5*/f32[8,768]{1,0:T(8,128)}) custom-call(f32[256,768]{1,0:T(8,128)} %refs_0_.1, f32[2,256,768]{2,1,0:T(8,128)} %get-tuple-element.51.refs_1_, ...), custom_call_target="tpu_custom_call" | custom-call | flops 24000000000 | bytes 60000000 | tf_op jit(solution)/shard_map/backward/pallas_call | solution.py:1234
  378.4 0.8 slice.47
  380.0 1.1 copy.84
  381.0 0.7 slice_bitcast_fusion.4
  381.8 0.8 reshape.123
  382.6 3.6 add_multiply_fusion.2
  386.6 1.0 copy-done
  387.6 1.1 pad_maximum_fusion
  389.3 1.1 copy.74
  390.4 2.3 reshape.121
  392.8 2.1 copy.75
  394.9 0.8 maximum_bitcast_fusion
  395.6 1.5 copy.76
  397.2 2.8 reshape.122
  399.9 3.6 add_multiply_fusion.3
  403.6 5.9 %add_multiply_fusion.1 = (f32[2,96,2,768]{3,2,1,0:T(2,128)}, f32[2,96,2,768]{3,2,1,0:T(2,128)}, f32[2,96,2,768]{3,2,1,0:T(2,128)}, f32[2,96,2,768]{3,2,1,0:T(2,128)}) fusion(f32[2,96,2,768]{3,2,1,0:T(2,128)S(1)} %copy-done.14, f32[2,96,2,768]{3,2,1,0:T(2,128)S(1)} %copy-done.5, f32[2,96,2,768]{3,2,1,0:T(2,128)S(1)} %reshape.123, ...), kind=kLoop, calls=%fused_computation.11 | loop fusion | flops 4718592 | bytes 10616832 | tf_op jit(solution)/shard_map/add | solution.py:1258
  409.6 4.1 add_multiply_fusion
  413.7 0.7 copy.89
  414.4 0.9 copy.90
  415.3 0.8 copy.91
  (66 shorter events, 3.8 us)
Async XLA Ops:
  0.7 8.5 %copy-start.4 = (f32[2,96,2,768]{3,2,1,0:T(2,128)S(1)}, f32[2,96,2,768]{3,2,1,0:T(2,128)}, u32[]{:S(2)}) copy-start(f32[2,96,2,768]{3,2,1,0:T(2,128)} %param.36) | copy-start | bytes 3538948
  3.9 2.4 copy-start.20
  8.2 2.6 copy-start.1
  190.9 188.3 %copy-start.21 = (f32[2,2,96]{2,1,0:T(2,128)S(1)}, f32[2,2,96]{2,1,0:T(2,128)}, u32[]{:S(2)}) copy-start(f32[2,2,96]{2,1,0:T(2,128)} %param.44) | copy-start | bytes 4612
  191.0 188.3 %copy-start.22 = (f32[2,2,96]{2,1,0:T(2,128)S(1)}, f32[2,2,96]{2,1,0:T(2,128)}, u32[]{:S(2)}) copy-start(f32[2,2,96]{2,1,0:T(2,128)} %param.47) | copy-start | bytes 4612
  191.0 188.3 %copy-start.23 = (f32[2,2,96]{2,1,0:T(2,128)S(1)}, f32[2,2,96]{2,1,0:T(2,128)}, u32[]{:S(2)}) copy-start(f32[2,2,96]{2,1,0:T(2,128)} %param.46) | copy-start | bytes 4612
  191.0 188.3 %copy-start.24 = (f32[2,2,96]{2,1,0:T(2,128)S(1)}, f32[2,2,96]{2,1,0:T(2,128)}, u32[]{:S(2)}) copy-start(f32[2,2,96]{2,1,0:T(2,128)} %param.45) | copy-start | bytes 4612
  378.4 3.4 copy-start.13
  380.0 2.6 copy-start.7
  380.0 2.6 copy-start.8
  382.6 21.0 %copy-start.6 = (f32[2,96,2,768]{3,2,1,0:T(2,128)}, f32[2,96,2,768]{3,2,1,0:T(2,128)S(1)}, u32[]{:S(2)}) copy-start(f32[2,96,2,768]{3,2,1,0:T(2,128)S(1)} %reshape.123) | copy-start | bytes 3538948
  382.6 3.6 copy-start.17
  386.4 1.3 copy-start
  387.6 1.7 slice-start
  399.9 3.6 copy-start.5
  399.9 3.6 copy-start.14
  399.9 3.6 copy-start.15
  399.9 3.6 copy-start.16
  403.6 6.0 %copy-start.2 = (f32[2,96,2304]{2,1,0:T(8,128)S(1)}, f32[2,96,2304]{2,1,0:T(8,128)}, u32[]{:S(2)}) copy-start(f32[2,96,2304]{2,1,0:T(8,128)} %param.28) | copy-start | bytes 5308420
  403.6 6.0 %copy-start.3 = (f32[2,96,2304]{2,1,0:T(8,128)S(1)}, f32[2,96,2304]{2,1,0:T(8,128)}, u32[]{:S(2)}) copy-start(f32[2,96,2304]{2,1,0:T(8,128)} %reshape.122) | copy-start | bytes 5308420
  403.6 6.0 %copy-start.10 = (f32[2,96,2304]{2,1,0:T(8,128)S(1)}, f32[2,96,2304]{2,1,0:T(8,128)}, u32[]{:S(2)}) copy-start(f32[2,96,2304]{2,1,0:T(8,128)} %param.31) | copy-start | bytes 5308420
  403.6 6.0 %copy-start.11 = (f32[2,96,2304]{2,1,0:T(8,128)S(1)}, f32[2,96,2304]{2,1,0:T(8,128)}, u32[]{:S(2)}) copy-start(f32[2,96,2304]{2,1,0:T(8,128)} %param.30) | copy-start | bytes 5308420
  403.6 5.9 %copy-start.12 = (f32[2,96,2304]{2,1,0:T(8,128)S(1)}, f32[2,96,2304]{2,1,0:T(8,128)}, u32[]{:S(2)}) copy-start(f32[2,96,2304]{2,1,0:T(8,128)} %param.29) | copy-start | bytes 5308420
  409.6 4.1 copy-start.19
  409.6 4.8 %copy-start.18 = (f32[256,768]{1,0:T(8,128)S(1)}, f32[256,768]{1,0:T(8,128)}, u32[]{:S(2)}) copy-start(f32[256,768]{1,0:T(8,128)} %get-tuple-element.138) | copy-start | bytes 2359300
  413.7 1.6 copy-start.9

commit v3 on v2

--- a/solution.py
+++ b/solution.py
@@ -14,6 +14,8 @@
 STEP = 10
 GROUP = 4
 DEPTH = 4
+LEAD = 1
+PIECES = 4
 OWN_HEADS = HEADS // GROUP
 TILE = 2 * HEAD_DIM
 PROJ = 5 * TILE
@@ -113,9 +115,7 @@
         z, x = spread.z, spread.x
         own = source.at[layer] if cols is None else source.at[layer, :, cols]
         place = self.view(z, x)
-        self.local = pltpu.make_async_copy(
-            source.at[layer], target.at[layer, spread.rows(2 * z + x)], local
-        )
+        self.local = pltpu.make_async_copy(own, place, local)
         self.beside = self.send(own, place, 0, 0, 2 * z + 1 - x)
         self.up = self.send(own, place, 1, 1 + z, 2 * jnp.minimum(z + 1, DEPTH - 1) + x)
         self.down = self.send(own, place, 2, 1 + z, 2 * jnp.maximum(z - 1, 0) + x)
@@ -161,12 +161,9 @@
             count -= 1
             arrive, over, along, comes, goes = self.hop(*self.todo.pop(0))
 
-            def receive():
-                arrive.wait_recv()
-                over.start()
-
-            pl.when(comes)(receive)
+            pl.when(comes)(arrive.wait_recv)
             pl.when(goes)(along.start)
+            pl.when(comes)(over.start)
 
     def wait(self):
         self.serve()
@@ -193,6 +190,8 @@
         me, mate, across, far, core = where
         cols = pl.ds(pl.multiple_of(core * half, half), half)
         super().__init__(source, target, layer, piece, sems, local, spread, cols)
+        here = spread.rows(2 * spread.z + spread.x)
+        self.local = pltpu.make_async_copy(source.at[layer], target.at[layer, here], local)
         self.swap = []
         for step in range(DEPTH):
             z = lax.rem(spread.z + step, DEPTH)
@@ -435,19 +434,25 @@
     ff = hid.shape[2]
     spread = Spread(wq_in.shape[1]) if spreading else None
     weights = []
+    parts = (
+        (wq_in, wq, None), (wo_in, wo, None), (wg_in, wg, None), (wd_in, wd, None),
+    )
     for layer in range(LAYERS):
-        for number, (source, target) in enumerate(((wq_in, wq), (wo_in, wo), (wg_in, wg), (wd_in, wd))):
+        for number, (source, target, cols) in enumerate(parts):
             local = wsems.at[layer, number]
+            piece = PIECES * layer + number
             if not spreading:
+                if cols is not None:
+                    source, target = source.at[:, :, cols], target.at[:, :, cols]
                 weights.append(pltpu.make_async_copy(source.at[layer], target.at[layer], local))
             elif number == 1:
                 weights.append(
-                    HalfGather(source, target, layer, 4 * layer + 1, dsems, local, spread,
+                    HalfGather(source, target, layer, piece, dsems, local, spread,
                                wo.shape[2] // 2, ssems, where)
                 )
             else:
                 weights.append(
-                    WeightGather(source, target, layer, 4 * layer + number, dsems, local, spread)
+                    WeightGather(source, target, layer, piece, dsems, local, spread, cols)
                 )
     xf[0, rows_of(me, size, size), :] = tok[...]
     greet(mate, across, None, spread)
@@ -460,7 +465,8 @@
             gains[-1].start()
     else:
         gain[...] = gain_in[...]
-    for item in weights:
+    ahead = LEAD if spreading else len(weights)
+    for item in weights[:ahead]:
         item.start()
 
     def gain_stage(stage):
@@ -479,13 +485,15 @@
             for copy in gains:
                 copy.wait_send()
 
-    def serve(layer, number, count=2 * DEPTH):
-        if spreading and layer < LAYERS:
-            item = weights[4 * layer + number]
-            if number == 1:
-                item.share()
-            else:
-                item.serve(count)
+    queue = [(k, hop) for k in range(len(weights)) for hop in range(6)] if spreading else []
+
+    def pump(count):
+        for number in range(min(count, len(queue))):
+            k, hop = queue.pop(0)
+            if hop == 0 and k + ahead < len(weights):
+                weights[k + ahead].start()
+            weights[k].serve(1)
+
     pending = []
     stores = []
 
@@ -500,10 +508,9 @@
     low_mask, high_mask = half_masks()
 
     for layer in range(LAYERS):
-        weights[4 * layer].wait()
-        serve(layer, 1)
         if layer == 0:
-            gain_stage(0)
+            pump(12)
+        weights[PIECES * layer].wait()
 
         def project(block, layer=layer):
             rows = rows_of(block, size, size)
@@ -520,9 +527,13 @@
         row_gather.wait_mate()
         project(mate)
         row_gather.wait_across()
+        if layer:
+            pump(2)
         project(across)
         row_gather.wait_far()
         project(far)
+        if layer == 0:
+            gain_stage(0)
         pending.append(row_gather)
         store(0, layer, xf, xf_out)
         store(1, layer, qkv, qkv_out)
@@ -568,7 +579,9 @@
             if head:
                 sends[-2].wait_recv()
                 forwards[-1].start()
-            serve(layer, 2, 2)
+            if spreading and head == 0:
+                weights[PIECES * layer + 1].share()
+            pump(2)
             sends += [to_across, to_mate]
             forwards.append(onward)
         sends[-2].wait_recv()
@@ -578,11 +591,13 @@
             forwards[head].wait_recv()
         store(2, layer, lse, lse_out)
         store(3, layer, att, att_out)
-        serve(layer, 3)
+        pump(6 - 2 * layer)
         if layer == 0:
             gain_stage(1)
-        for number in range(1, 4):
-            weights[4 * layer + number].wait()
+        for number in range(1, PIECES):
+            weights[PIECES * layer + number].wait()
+        for number, held in enumerate((wq, wo, wg, wd)):
+            store(12 + number, layer, held, weight_outs[number])
 
         def feed(block, keep, layer=layer):
             rows = rows_of(block, size, size)
@@ -604,15 +619,19 @@
 
         scatter = Scatter(part, layer, got, layer, sems, 15, where)
         scatter.send_far(feed(far, False))
+        pump(2)
         scatter.send_across(feed(across, False))
+        pump(2)
         scatter.send_mate(feed(mate, False))
+        pump(2)
         own_part = feed(me, True)
-        serve(layer + 1, 0)
+        pump(2)
         store(4, layer, flow, flow_out)
         store(5, layer, gu, gu_out)
         store(6, layer, hid, hid_out)
         store(7, layer, n1, n1_out)
         store(8, layer, s1, s1_out)
+        pump(2)
         ffn = scatter.total(own_part)
         pending.append(scatter)
         normed, inverse = normed_rows(first[...] + ffn)
@@ -625,6 +644,7 @@
             xf[layer + 1, rows_of(me, size, size), :] = result
             row_gather = Gather(xf, layer + 1, layer + 1, sems, 0, size, where)
             row_gather.start()
+            pump(2)
         else:
             act[...] = result
             copy = pltpu.make_async_copy(act, act_out, osems.at[0, 11])
@@ -632,9 +652,6 @@
             stores.append(copy)
         for copy in sends + forwards:
             copy.wait_send()
-        if spreading:
-            for number, held in enumerate((wq, wo, wg, wd)):
-                store(12 + number, layer, held, weight_outs[number])
     if spreading:
         pending += weights
     for item in pending:
@@ -932,7 +949,7 @@
         if layer == 0:
             weigh_out(layer)
             gain_stage(1)
-        add("d", layer)
+            add("d", layer)
         total("q", layer + 1)
         total("o", layer + 1)
 
@@ -970,15 +987,14 @@
 
             lax.fori_loop(0, seq // size, attend, 0)
             if head == 0:
-                add("g", layer)
+                add("g" if layer == 0 else "d", layer)
                 for share in shares:
                     share.serve()
-            if head == 1 and layer == 0:
-                add("o", layer)
+            if head == 1 and layer:
+                add("g", layer)
             if layer == 0 and head < 2:
                 gain_stage(2 + head)
 
-        add("u", layer)
 
         def unrotate(i, carry):
             rows = rows_of(i, size, size)
@@ -993,6 +1009,8 @@
             return carry
 
         lax.fori_loop(0, seq // size, unrotate, 0)
+        if layer == 0:
+            add("u", layer)
         load("qkv", layer - 1)
         load("lse", layer - 1)
         loads["wq"].wait()
@@ -1020,6 +1038,10 @@
 
         lax.fori_loop(0, feats // 256, qkv_weight, 0)
         begin("q", layer)
+        if layer:
+            add("u", layer)
+        else:
+            add("o", layer)
         load("flow", layer - 1)
         if layer:
             weigh_out(layer)
@@ -1048,6 +1070,125 @@
             copy = pltpu.make_async_copy(*held, osems.at[1, number])
             copy.start()
             copy.wait()
+
+
+RATES = ((0.03, 0.01), (0.5, 0.01), (0.03, 0.01), (0.02, 0.01), (0.6, 0.0))
+
+
+def adam_step(weight, first, second, average, gradient, rate, decay):
+    first_new = beta_first * first + (1.0 - beta_first) * gradient
+    second_new = beta_second * second + (1.0 - beta_second) * gradient * gradient
+    first_hat = first_new / (1.0 - beta_first**STEP)
+    second_hat = second_new / (1.0 - beta_second**STEP)
+    weight_new = weight - rate * (
+        first_hat / (jnp.sqrt(second_hat) + adam_epsilon) + decay * weight
+    )
+    average_new = average_decay * average + (1.0 - average_decay) * weight_new
+    return first_new, second_new, weight_new, average_new
+
+
+def adam_kernel(*refs):
+    states = [refs[4 * f:4 * f + 4] for f in range(5)]
+    grads = refs[20:25]
+    outs = [refs[25 + 5 * f:30 + 5 * f] for f in range(5)]
+    (qs, os, ds, gs, qg, og, gg, qb, ob, gb, db, gsems, isems, usems) = refs[50:]
+    width = ob.shape[3]
+    for number, target in enumerate((qs, os, gs, ds)):
+        pltpu.make_async_copy(grads[number], target, gsems.at[number]).start()
+    chunks = []
+    for family, held, grad in ((3, db, ds), (2, gb, gg), (1, ob, og), (0, qb, qg)):
+        for layer in range(LAYERS):
+            for part in range(3 if family == 0 else 1):
+                spot = 3 * layer + part if family == 0 else layer
+                chunks.append((family, held, grad, layer, part, spot))
+
+    def view(ref, family, layer, part):
+        if family:
+            return ref.at[layer]
+        return ref.at[layer, :, pl.ds(part * width, width)]
+
+    arrivals = []
+    for number, (family, held, grad, layer, part, spot) in enumerate(chunks):
+        copies = [
+            pltpu.make_async_copy(
+                view(states[family][k], family, layer, part), held.at[k, spot], isems.at[number, k]
+            )
+            for k in range(4)
+        ]
+        for copy in copies:
+            copy.start()
+        arrivals.append(copies)
+
+    def wait_grad(number, target):
+        pltpu.make_async_copy(grads[number], target, gsems.at[number]).wait()
+
+    gain = [ref[...] for ref in states[4]]
+    gradient = grads[4][...]
+    new = adam_step(*gain, gradient, *RATES[4])
+    for ref, value in zip(outs[4], (gradient,) + new):
+        ref[...] = value
+
+    low = lane_iota((qs.shape[2], TILE)) < HEAD_DIM
+    leaving = []
+    for number, (family, held, grad, layer, part, spot) in enumerate(chunks):
+        first_of = layer == 0 and part == 0
+        if family == 3 and first_of:
+            wait_grad(3, ds)
+        if family == 2:
+            if first_of:
+                wait_grad(2, gs)
+            for half in range(2):
+                gg[layer, :, half, :] = gs[layer, :, half * width:(half + 1) * width]
+        if family == 1:
+            if first_of:
+                wait_grad(1, os)
+            half = width // 2
+            og[layer, :, :half] = os[layer, 0].astype(f32)
+            og[layer, :, half:] = os[layer, 1].astype(f32)
+        if family == 0:
+            if first_of:
+                wait_grad(0, qs)
+
+            def pair(j):
+                return qs[layer, j, :, part * TILE:(part + 1) * TILE].astype(f32)
+
+            def last(j, upper):
+                tile = 4 if part == 2 else 3
+                value = qs[layer, j, :, tile * TILE:(tile + 1) * TILE].astype(f32)
+                return value if upper == (part > 0) else pltpu.roll(value, HEAD_DIM, 1)
+
+            for j in (0, 2):
+                turned = pltpu.roll(pair(j + 1), HEAD_DIM, 1)
+                tiles = (
+                    pair(j),
+                    jnp.where(low, last(j, False), turned),
+                    jnp.where(low, turned, last(j + 1, True)),
+                )
+                for k, value in enumerate(tiles):
+                    start = (3 * (j // 2) + k) * TILE
+                    qg[spot, :, start:start + TILE] = value
+        for copy in arrivals[number]:
+            copy.wait()
+        rows = 32
+
+        def body(i, carry, family=family, held=held, grad=grad, spot=spot):
+            at = pl.ds(pl.multiple_of(i * rows, rows), rows)
+            values = [held[k, spot, at] for k in range(4)]
+            first, second, weight, average = adam_step(*values, grad[spot, at], *RATES[family])
+            for k, value in enumerate((weight, first, second, average)):
+                held[k, spot, at] = value
+            return carry
+
+        lax.fori_loop(0, ob.shape[2] // rows, body, 0)
+        sources = (grad.at[spot],) + tuple(held.at[k, spot] for k in (1, 2, 0, 3))
+        for k, source in enumerate(sources):
+            copy = pltpu.make_async_copy(
+                source, view(outs[family][k], family, layer, part), usems.at[number, k]
+            )
+            copy.start()
+            leaving.append(copy)
+    for copy in leaving:
+        copy.wait()
 
 
 def pack_documents(length_row, mask_row):
@@ -1135,9 +1276,9 @@
         pltpu.VMEM((LAYERS, 3, size, feats), bf16),
         pltpu.VMEM((LAYERS, 3, size, feats), bf16),
         pltpu.SemaphoreType.DMA((2, LAYERS, 18)),
-        pltpu.SemaphoreType.DMA((LAYERS, 4)),
+        pltpu.SemaphoreType.DMA((LAYERS, PIECES)),
         pltpu.SemaphoreType.DMA((LAYERS, 16)),
-        pltpu.SemaphoreType.DMA((2, 4 * LAYERS, 3 + 2 * DEPTH)),
+        pltpu.SemaphoreType.DMA((2, PIECES * LAYERS, 3 + 2 * DEPTH)),
         pltpu.SemaphoreType.DMA((2, LAYERS, 7)),
         pltpu.VMEM((2, 8, feats), f32),
         pltpu.VMEM((DEPTH, 8, feats), f32),
@@ -1247,6 +1388,42 @@
     )(cotangent, *loaded, gain, *tables)
 
 
+def run_adam(states, grads):
+    outs = []
+    for family in range(5):
+        shape = jax.ShapeDtypeStruct(states[4 * family].shape, f32)
+        outs += [shape] * 5
+    layers, own, _, width = states[8].shape
+    scratch = [
+        pltpu.VMEM(grads[0].shape, bf16),
+        pltpu.VMEM(grads[1].shape, bf16),
+        pltpu.VMEM(grads[3].shape, f32),
+        pltpu.VMEM(grads[2].shape, f32),
+        pltpu.VMEM((3 * layers, own, width), f32),
+        pltpu.VMEM((layers, own, width), f32),
+        pltpu.VMEM((layers, own, 2, width), f32),
+        pltpu.VMEM((4, 3 * layers, own, width), f32),
+        pltpu.VMEM((4, layers, own, width), f32),
+        pltpu.VMEM((4, layers, own, 2, width), f32),
+        pltpu.VMEM((4, layers, own, width), f32),
+        pltpu.SemaphoreType.DMA((4,)),
+        pltpu.SemaphoreType.DMA((6 * layers, 4)),
+        pltpu.SemaphoreType.DMA((6 * layers, 5)),
+    ]
+    return pl.pallas_call(
+        adam_kernel,
+        out_shape=outs,
+        in_specs=[ANY] * 16 + [VMEM] * 4 + [ANY] * 4 + [VMEM],
+        out_specs=[ANY] * 20 + [VMEM] * 5,
+        scratch_shapes=scratch,
+        compiler_params=pltpu.CompilerParams(vmem_limit_bytes=VMEM_LIMIT),
+        cost_estimate=pl.CostEstimate(
+            flops=2 * 10**7, bytes_accessed=37 * 10**6, transcendentals=10**6
+        ),
+        name="adam",
+    )(*states, *grads)
+
+
 def adamw(weight, first, second, average, gradient, rate, decay):
     first_new = beta_first * first + (1.0 - beta_first) * gradient
     second_new = beta_second * second + (1.0 - beta_second) * gradient * gradient
@@ -1312,10 +1489,17 @@
     backward = run_backward(spreading, cotangent, kept, weights, gain, tables)
     if spreading:
         input_grad, gq, go, gd, gg, gain_sum = backward
-        gq, go = gq.transpose(1, 0, 2, 3), go.transpose(1, 0, 2, 3)
         gain_grad = lax.dynamic_slice_in_dim(
             gain_sum[:2 * LAYERS].reshape(LAYERS, 2, -1), lax.axis_index("dp") * own, own, 2
         )
+        states = (
+            qkv_weight, qkv_first, qkv_second, qkv_average,
+            out_weight, out_first, out_second, out_average,
+            gate_up_weight, gate_up_first, gate_up_second, gate_up_average,
+            down_weight, down_first, down_second, down_average,
+            norm_gain, gain_first, gain_second, gain_average,
+        )
+        return (act, input_grad, *run_adam(states, (gq, go, gg, gd, gain_grad)))
     else:
         input_grad, gq, go, gd, gg, gain_sum = backward
         gq, go, gg, gd = [

time: 424 us -> 384 us (0.906)
  other arithmetic: 30.1 us -> 10.2 us
  local copies, waits for them, and re-layouts: 23.7 us -> 10.2 us
  Pallas kernels: 361 us -> 355 us
    pallas_call x1, Pallas kernels: 174 us -> 151 us  [run_forward(): pl.pallas_call(functools.partial(forward_kernel, spreading), out_shape=[j...]
    add x5 -> x0, other arithmetic: 17.9 us -> none  [adamw(): average_new = average_decay * average + (1.0 - average_decay) * weight_new]
    pallas_call x0 -> x1, Pallas kernels: none -> 16 us  [run_adam(): pl.pallas_call(adam_kernel, out_shape=outs, in_specs=[ANY] * 16 + [VMEM]...]
    reshape x3 -> x0, local copies, waits for them, and re-layouts: 5.87 us -> none  [the longest x1 2.76 us: whole_projection(): full.transpose(1, 2, 3, 0, 4).reshape(layers, rows, 3 * HEADS * HEAD_DIM)]
where the time goes in v3:
time: 384 us; the launch traced here: 377 us
  Pallas kernels  355 us (92%)
  local copies, waits for them, and re-layouts  10.2 us (3%)
  other arithmetic  10.2 us (3%)
    pallas_call x1, Pallas kernels, run_backward(): pl.pallas_call(functools.partial(backward_kernel, spreading, tuple(names...  188 us
    pallas_call x1, Pallas kernels, run_forward(): pl.pallas_call(functools.partial(forward_kernel, spreading), out_shape=[j...  151 us
    pallas_call x1, Pallas kernels, run_adam(): pl.pallas_call(adam_kernel, out_shape=outs, in_specs=[ANY] * 16 + [VMEM]...  16 us

profile of v3, /device:TPU:0, one launch (start us, length us, event | category | flops | bytes accessed | tf_op | source)
XLA Modules:
  0.0 376.7 jit_solution(7656693163526218148)
XLA Ops:
  0.7 0.0 copy-start.1
  0.7 0.9 reduce-window.8
  1.6 0.1 convert_reduce_fusion
  1.7 0.7 subtract_convert_fusion
  2.4 1.5 dynamic_update_slice.3.gain_in
  3.9 0.0 copy-start.3
  3.9 0.6 broadcast_in_dim.42.doc_queries.refs_20_
  4.5 1.8 convert_element_type.32.wo_in
  6.4 0.0 copy-done.3
  6.4 1.8 convert_element_type.35.wd_in
  8.2 0.0 copy-start
  8.2 1.0 broadcast_in_dim.41.doc_keys.refs_19_
  9.2 0.0 copy-done.1
  9.2 0.4 convert_element_type.33
  9.6 1.2 convert_element_type.34.wg_in
  10.8 0.0 copy-done
  10.8 0.5 reshape.107
  11.2 0.3 constant_dynamic-slice_fusion.1
  11.7 0.8 concatenate.9.wq_in
  12.5 1.9 fusion
  14.4 1.3 pad_maximum_fusion.1.sin_rows.refs_18_
  15.7 1.3 pad_maximum_fusion.cos_rows.refs_17_
  16.9 150.6 %forward.1 = (bf16[256,768]{1,0:T(8,128)(2,1)}, bf16[2,1024,768]{2,1,0:T(8,128)(2,1)}, bf16[2,1024,640]{2,1,0:T(8,128)(2,1)}, f32[2,8,1024]{2,1,0:T(8,128)}, bf1...) custom-call(bf16[256,768]{1,0:T(8,128)(2,1)} %tok.1, ...), custom_call_target="tpu_custom_call" | custom-call | flops 12000000000 | bytes 60000000 | tf_op jit(solution)/shard_map/forward/pallas_call | solution.py:1287
  167.5 188.4 %backward.1 = (f32[256,768]{1,0:T(8,128)}, bf16[2,4,96,640]{3,2,1,0:T(8,128)(2,1)}, bf16[2,2,96,384]{3,2,1,0:T(8,128)(2,1)}, f32[2,96,768]{2,1,0:T(8,128)}, f32[2,96,1536]{2,1,0:T(8,128)}, /*index=5*/f32[8,768]{1,0:T(8,128)}) custom-call(f32[256,768]{1,0:T(8,128)} %refs_0_.2, f32[2,256,768]{2,1,0:T(8,128)} %get-tuple-element.76.refs_1_, ...), custom_call_target="tpu_custom_call" | custom-call | flops 24000000000 | bytes 60000000 | tf_op jit(solution)/shard_map/backward/pallas_call | solution.py:1375
  356.0 0.7 slice.23
  356.7 0.7 constant_dynamic-slice_fusion.refs_24_
  357.4 0.0 copy-start.2
  357.4 16.0 %adam.1 = (f32[2,96,2304]{2,1,0:T(8,128)}, f32[2,96,2304]{2,1,0:T(8,128)}, f32[2,96,2304]{2,1,0:T(8,128)}, f32[2,96,2304]{2,1,0:T(8,128)}, f32[2,96,2304]{2,1,0:...) custom-call(f32[2,96,2304]{2,1,0:T(8,128)} %refs_0_.3, ...), custom_call_target="tpu_custom_call" | custom-call | flops 20000000 | bytes 37000000 | tf_op jit(solution)/shard_map/adam/pallas_call | solution.py:1413
  373.4 0.0 copy-done.2
  373.4 0.7 copy.66
  374.2 2.1 copy.67
  (7 shorter events, 0.1 us)
Async XLA Ops:
  0.7 8.5 %copy-start.1 = (f32[2,96,2,768]{3,2,1,0:T(2,128)S(1)}, f32[2,96,2,768]{3,2,1,0:T(2,128)}, u32[]{:S(2)}) copy-start(f32[2,96,2,768]{3,2,1,0:T(2,128)} %refs_8_.1) | copy-start | bytes 3538948
  3.9 2.4 copy-start.3
  8.2 2.6 copy-start
  357.4 16.1 %copy-start.2 = (bf16[256,768]{1,0:T(8,128)(2,1)S(1)}, bf16[256,768]{1,0:T(8,128)(2,1)}, u32[]{:S(2)}) copy-start(bf16[256,768]{1,0:T(8,128)(2,1)} %get-tuple-element.160) | copy-start | bytes 1179652

commit v4 on v3

--- a/solution.py
+++ b/solution.py
@@ -668,13 +668,6 @@
     "bias", "dff", "dbr", "datt", "dproj", "dk", "dv", "dqt", "kt", "k2", "grad", "part", "got",
     "gq", "go", "gg", "gd", "sems", "lsems", "osems",
 )
-BACK_SPREAD = (
-    "gsum", "gpack", "gside", "gdeep", "gsems", "csems", "qshare", "oshare",
-    "near_d", "near_g", "near_u", "near_q", "near_o",
-    "apart_d", "apart_g", "apart_u", "apart_q", "apart_o",
-    "sum_d", "sum_g", "sum_u", "sum_q", "sum_o", "dsems",
-)
-
 
 def backward_kernel(spreading, names, *refs):
     r = dict(zip(names, refs))
@@ -720,22 +713,21 @@
     sums = {}
     shares = []
     pieces = dict(
-        d=gd.at[:, :], g=gg.at[:, :ff], u=gg.at[:, ff:], q=gq.at[:, :], o=go.at[:, :]
+        d=gd.at[:, :], g=gg.at[:, :ff], u=gg.at[:, ff:],
+        a=gq.at[:, :3 * TILE], b=gq.at[:, 3 * TILE:], o=go.at[:, :],
     )
     gsum = r["gsum"] if spreading else r["gain_out"]
     gsum[...] = jnp.zeros_like(gsum)
 
     def begin(name, layer):
         if not spreading:
-            if name == "u":
-                store(2, layer, gg, r["g_out"])
-            elif name != "g":
-                number = "qogd".index(name)
-                store(number, layer, (gq, go, gg, gd)[number], r[name + "_out"])
+            if name not in "ga":
+                number = "boud".index(name)
+                store(number, layer, (gq, go, gg, gd)[number], r["qogd"[number] + "_out"])
             return
-        index = "dguqo".index(name)
+        index = "dguabo".index(name)
         item = WeightSum(
-            pieces[name], r["near_" + name], r["apart_" + name], 5 * layer + index, r["dsems"],
+            pieces[name], r["near_" + name], r["apart_" + name], 6 * layer + index, r["dsems"],
             spread, (r["csems"].at[0, index], r["csems"].at[1, index]),
             layer < LAYERS - 1, layer > 0, r["sum_" + name],
         )
@@ -750,14 +742,14 @@
         if not spreading or (name, layer) not in sums:
             return
         result = sums[name, layer].total()
-        if name == "q":
-            share = Share(r["qshare"], layer, sems, 15, where)
+        if name in "ab":
+            share = Share(r[name + "share"], layer, sems, 15 if name == "a" else 18, where)
             share.start(result.astype(bf16))
             shares.append(share)
         elif name == "o":
             oshare = r["oshare"]
             oshare[layer, core] = result.astype(bf16)
-            copy = push(oshare.at[layer, core], oshare.at[layer, core], sems, layer, 18, mate)
+            copy = push(oshare.at[layer, core], oshare.at[layer, core], sems, layer, 21, mate)
             copy.start()
             oshares.append(copy)
         elif name == "d":
@@ -768,8 +760,8 @@
 
     def ready(name, layer):
         if not spreading:
-            if name != "u":
-                stored("qogd".index(name))
+            if name not in "ub":
+                stored("aogd".index(name))
         elif (name, layer + 1) in sums:
             sums[name, layer + 1].finish()
 
@@ -839,8 +831,9 @@
         gather.start()
         for name in ("wd", "gu", "wg"):
             loads[name].wait()
-
-        def feed_back(block, layer=layer):
+        add("o", layer + 1)
+
+        def feed_back(block):
             rows = rows_of(block, size, size)
             grad_hidden = dot(dff[0, rows, :], wd[...])
             gate = gu[rows, :ff].astype(f32)
@@ -860,26 +853,42 @@
         gather.wait_mate()
         scatter.send_mate(feed_back(mate))
         gather.wait_across()
-        across_part = feed_back(across)
+        loads["hid"].wait()
+        add("a", layer + 1)
         gather.wait_far()
-        scatter.send_far(feed_back(far))
-        scatter.send_across(across_part)
-        load("wd", layer - 1)
-        load("wg", layer - 1)
-        loads["hid"].wait()
-        add("q", layer + 1)
         ready("d", layer)
 
-        def down_weight(i, carry, layer=layer):
+        def down_weight(i, carry):
             cols = rows_of(i, 256, 256)
             gd[cols, :] = dot_tn(dff[0, :, cols], hid[...]).astype(bf16)
             return carry
 
         lax.fori_loop(0, feats // 256, down_weight, 0)
         begin("d", layer)
+        scatter.send_far(feed_back(far))
+        scatter.send_across(feed_back(across))
         gather.finish()
         load("hid", layer - 1)
-        add("o", layer + 1)
+        load("wd", layer - 1)
+        load("wg", layer - 1)
+        add("b", layer + 1)
+        loads["flow"].wait()
+        for name, first_col in (("g", 0), ("u", ff)):
+            ready(name, layer)
+
+            def gate_up_weight(i, carry, first_col=first_col):
+                cols = rows_of(i, 256, 256)
+                gg[cols, first_col:first_col + ff] = dot_tn(
+                    flow[:, cols], gu[:, first_col:first_col + ff]
+                ).astype(bf16)
+                return carry
+
+            lax.fori_loop(0, feats // 256, gate_up_weight, 0)
+            begin(name, layer)
+        load("gu", layer - 1)
+        load("xf", layer)
+        for name in "dgu":
+            total(name, layer + 1)
 
         dfirst = grad[...] + scatter.total(own_part)
         loads["n1"].wait()
@@ -891,43 +900,10 @@
         dbr[layer, rows_of(me, size, size), :] = dr.astype(bf16)
         gather = Gather(dbr, layer, layer, sems, 9, size, where)
         gather.start()
-        loads["flow"].wait()
-
         if layer == 0:
             gain_stage(0)
-        for name, first_col in (("g", 0), ("u", ff)):
-            ready(name, layer)
-
-            def gate_up_weight(i, carry, first_col=first_col):
-                cols = rows_of(i, 256, 256)
-                gg[cols, first_col:first_col + ff] = dot_tn(
-                    flow[:, cols], gu[:, first_col:first_col + ff]
-                ).astype(bf16)
-                return carry
-
-            lax.fori_loop(0, feats // 256, gate_up_weight, 0)
-            begin(name, layer)
-        load("gu", layer - 1)
-        load("xf", layer)
-        for name in "dgu":
-            total(name, layer + 1)
-
-        loads["wo"].wait()
-
-        def weigh_out(layer):
-            loads["att"].wait()
-            ready("o", layer)
-
-            def out_weight(i, carry):
-                rows = rows_of(i, 256, 256)
-                half = feats // 2
-                cols = pl.ds(pl.multiple_of(core * half, half), half)
-                go[rows, :] = dot(att[rows, :], dbr[layer, :, cols]).astype(bf16)
-                return carry
-
-            lax.fori_loop(0, feats // 256, out_weight, 0)
-            begin("o", layer)
-            load("att", layer - 1)
+        for name in ("wo", "qkv", "lse"):
+            loads[name].wait()
 
         def att_back(block, layer=layer):
             rows = rows_of(block, size, size)
@@ -937,39 +913,21 @@
                     dbr[layer, rows, :], wo[spot, :]
                 ).astype(bf16)
 
-        att_back(me)
-        gather.wait_mate()
-        att_back(mate)
-        gather.wait_across()
-        att_back(across)
-        gather.wait_far()
-        att_back(far)
-        pending.append(gather)
-        load("wo", layer - 1)
-        if layer == 0:
-            weigh_out(layer)
-            gain_stage(1)
-            add("d", layer)
-        total("q", layer + 1)
-        total("o", layer + 1)
-
-        loads["qkv"].wait()
-        loads["lse"].wait()
         kt[0] = qkv[:, TILE:2 * TILE].T
         kt[1] = qkv[:, 3 * TILE:4 * TILE].T
         k2[...] = pltpu.roll(qkv[:, 3 * TILE:4 * TILE].astype(f32), HEAD_DIM, 1).astype(bf16)
         dk[...] = jnp.zeros_like(dk)
         dv[...] = jnp.zeros_like(dv)
-        for head in range(OWN_HEADS):
+
+        def attend(head, first, second):
             tile = head // 2
             query_tile = (0, 0, 3)[head]
             value_tile = (2, 2, 4)[head]
             query_mask = (low_mask, high_mask, low_mask)[head]
             value_mask = (low_mask, high_mask, high_mask)[head]
 
-            def attend(i, carry, head=head, tile=tile, query_tile=query_tile, value_tile=value_tile,
-                       query_mask=query_mask, value_mask=value_mask):
-                rows = rows_of(i, size, size)
+            def body(i, carry):
+                rows = rows_of(first + i * (second - first), size, size)
                 queries = qkv[rows, query_tile * TILE:(query_tile + 1) * TILE] * query_mask
                 keys = k2[...] if head == 2 else qkv[:, TILE:2 * TILE]
                 scores = dot_nt(keys, queries) * (score_scale * log2e) + bias[:, rows]
@@ -985,32 +943,83 @@
                 dqt[tile, spot:spot + HEAD_DIM, rows] = dot(keys_t, grad_scores)
                 return carry
 
-            lax.fori_loop(0, seq // size, attend, 0)
-            if head == 0:
-                add("g" if layer == 0 else "d", layer)
-                for share in shares:
-                    share.serve()
-            if head == 1 and layer:
-                add("g", layer)
-            if layer == 0 and head < 2:
-                gain_stage(2 + head)
-
-
-        def unrotate(i, carry):
+            lax.fori_loop(0, 2, body, 0)
+
+        att_back(me)
+        gather.wait_mate()
+        att_back(mate)
+        if layer == 0:
+            add("d", layer)
+        for head in range(OWN_HEADS):
+            attend(head, me, mate)
+        gather.wait_across()
+        att_back(across)
+        if layer == 0:
+            gain_stage(1)
+            add("g", layer)
+        else:
+            add("d", layer)
+        gather.wait_far()
+        att_back(far)
+        pending.append(gather)
+        load("wo", layer - 1)
+        loads["att"].wait()
+        ready("o", layer)
+
+        def out_weight(i, carry, layer=layer):
+            rows = rows_of(i, 256, 256)
+            half = feats // 2
+            cols = pl.ds(pl.multiple_of(core * half, half), half)
+            go[rows, :] = dot(att[rows, :], dbr[layer, :, cols]).astype(bf16)
+            return carry
+
+        lax.fori_loop(0, feats // 256, out_weight, 0)
+        begin("o", layer)
+        load("att", layer - 1)
+        for name in "oab":
+            total(name, layer + 1)
+        attend(0, across, far)
+        attend(1, across, far)
+        for share in shares:
+            share.serve()
+
+        def unrotate_pairs(i, carry):
             rows = rows_of(i, size, size)
             c, s = cos_rows[rows, :], -sin_rows[rows, :]
             dproj[rows, :TILE] = turn(dqt[0, :, rows].T * score_scale, c, s).astype(bf16)
             dproj[rows, TILE:2 * TILE] = turn(dk[0, rows, :] * score_scale, c, s).astype(bf16)
             dproj[rows, 2 * TILE:3 * TILE] = dv[0, rows, :].astype(bf16)
+            return carry
+
+        def unrotate_last(i, carry):
+            rows = rows_of(i, size, size)
+            c, s = cos_rows[rows, :], -sin_rows[rows, :]
             lower = lane_iota((size, TILE)) < HEAD_DIM
             mixed = jnp.where(lower, dqt[1, :, rows].T, pltpu.roll(dk[1, rows, :], HEAD_DIM, 1))
             dproj[rows, 3 * TILE:4 * TILE] = turn(mixed * score_scale, c, s).astype(bf16)
             dproj[rows, 4 * TILE:] = dv[1, rows, :].astype(bf16)
             return carry
 
-        lax.fori_loop(0, seq // size, unrotate, 0)
-        if layer == 0:
+        def weigh_projection(first, last):
+            def qkv_weight(i, carry):
+                cols = rows_of(i, 256, 256)
+                gq[cols, first:last] = dot_tn(xf[:, cols], dproj[:, first:last]).astype(bf16)
+                return carry
+
+            lax.fori_loop(0, feats // 256, qkv_weight, 0)
+
+        lax.fori_loop(0, seq // size, unrotate_pairs, 0)
+        loads["xf"].wait()
+        ready("a", layer)
+        weigh_projection(0, 3 * TILE)
+        begin("a", layer)
+        if layer:
+            add("g", layer)
+        else:
+            gain_stage(2)
             add("u", layer)
+        attend(2, across, far)
+        lax.fori_loop(0, seq // size, unrotate_last, 0)
         load("qkv", layer - 1)
         load("lse", layer - 1)
         loads["wq"].wait()
@@ -1022,38 +1031,36 @@
             scatters[-2].finish()
         scatter = Scatter(part, 1, got, 2 * layer + 1, sems, 6, where)
         scatters.append(scatter)
+        if layer == 0:
+            ready("b", layer)
+            weigh_projection(3 * TILE, PROJ)
+            begin("b", layer)
         scatter.send_far(input_part(far))
         scatter.send_across(input_part(across))
         scatter.send_mate(input_part(mate))
         own_part = input_part(me)
         load("wq", layer - 1)
-        loads["xf"].wait()
-
-        ready("q", layer)
-
-        def qkv_weight(i, carry, layer=layer):
-            cols = rows_of(i, 256, 256)
-            gq[cols, :] = dot_tn(xf[:, cols], dproj[...]).astype(bf16)
-            return carry
-
-        lax.fori_loop(0, feats // 256, qkv_weight, 0)
-        begin("q", layer)
         if layer:
+            ready("b", layer)
+            weigh_projection(3 * TILE, PROJ)
+            begin("b", layer)
             add("u", layer)
         else:
+            gain_stage(3)
             add("o", layer)
+            add("a", layer)
+            for name in "dg":
+                total(name, 0)
+            add("b", layer)
         load("flow", layer - 1)
-        if layer:
-            weigh_out(layer)
         grad[...] = grad[...] + scatter.total(own_part)
     input_copy = pltpu.make_async_copy(grad, r["ig_out"], osems.at[0, 4])
     input_copy.start()
-    for name in "dguo":
+    for name in "uoab":
         total(name, 0)
-    add("q", 0)
-    total("q", 0)
     if spreading:
-        shares[-1].serve()
+        for share in shares[-2:]:
+            share.serve()
     input_copy.wait()
     for item in pending + scatters[-2:]:
         item.finish()
@@ -1064,11 +1071,19 @@
     for copy in oshares:
         copy.wait()
     if spreading:
-        for name in "dguqo":
+        for name in "dguabo":
             sums[name, 0].finish()
-        for number, held in enumerate(((r["qshare"], r["q_out"]), (r["oshare"], r["o_out"]))):
-            copy = pltpu.make_async_copy(*held, osems.at[1, number])
-            copy.start()
+        q_out = r["q_out"]
+        ends = (
+            (r["ashare"], q_out.at[:, :, :, pl.ds(0, 3 * TILE)]),
+            (r["bshare"], q_out.at[:, :, :, pl.ds(3 * TILE, 2 * TILE)]),
+            (r["oshare"], r["o_out"]),
+        )
+        last = []
+        for number, held in enumerate(ends):
+            last.append(pltpu.make_async_copy(*held, osems.at[1, number]))
+            last[-1].start()
+        for copy in last:
             copy.wait()
 
 
@@ -1309,7 +1324,7 @@
     loaded = [n1, s1, n2, s2, xf, qkv, lse, att, flow, gu, hid, wq, wo, wg, wd]
     own = feats // (2 * DEPTH)
     half = feats // 2
-    widths = dict(d=ff, g=ff, u=ff, q=PROJ, o=half)
+    widths = dict(d=ff, g=ff, u=ff, a=3 * TILE, b=2 * TILE, o=half)
     if spreading:
         outs = dict(
             ig_out=((size, feats), f32),
@@ -1347,7 +1362,7 @@
         go=pltpu.VMEM((feats, half), bf16),
         gg=pltpu.VMEM((feats, 2 * ff), bf16),
         gd=pltpu.VMEM((feats, ff), bf16),
-        sems=pltpu.SemaphoreType.DMA((2, 2 * LAYERS, 19)),
+        sems=pltpu.SemaphoreType.DMA((2, 2 * LAYERS, 22)),
         lsems=pltpu.SemaphoreType.DMA((len(loaded),)),
         osems=pltpu.SemaphoreType.DMA((LAYERS, 5)),
         rows=pltpu.VMEM((seq, feats), bf16),
@@ -1362,10 +1377,11 @@
             gside=pltpu.VMEM((2, 8, feats), f32),
             gdeep=pltpu.VMEM((DEPTH, 8, feats), f32),
             gsems=pltpu.SemaphoreType.DMA((2, 1, 7)),
-            csems=pltpu.SemaphoreType.REGULAR((2, 5)),
-            qshare=pltpu.VMEM((LAYERS, GROUP, own, PROJ), bf16),
+            csems=pltpu.SemaphoreType.REGULAR((2, 6)),
+            ashare=pltpu.VMEM((LAYERS, GROUP, own, 3 * TILE), bf16),
+            bshare=pltpu.VMEM((LAYERS, GROUP, own, 2 * TILE), bf16),
             oshare=pltpu.VMEM((LAYERS, 2, own, half), bf16),
-            dsems=pltpu.SemaphoreType.DMA((2, 5 * LAYERS, 7)),
+            dsems=pltpu.SemaphoreType.DMA((2, 6 * LAYERS, 7)),
         )
         for name, width in widths.items():
             scratch["near_" + name] = pltpu.VMEM((DEPTH, own, width), bf16)

time: 384 us -> 363 us (0.945)
  the two profiles are of different devices: /device:TPU:0 before, /device:TPU:3 now
where the time goes in v4:
time: 363 us; the launch traced here: 356 us
  Pallas kernels  334 us (92%)
  local copies, waits for them, and re-layouts  10.4 us (3%)
  other arithmetic  10.2 us (3%)
    pallas_call x1, Pallas kernels, run_backward(): pl.pallas_call(functools.partial(backward_kernel, spreading, tuple(names...  167 us
    pallas_call x1, Pallas kernels, run_forward(): pl.pallas_call(functools.partial(forward_kernel, spreading), out_shape=[j...  151 us
    pallas_call x1, Pallas kernels, run_adam(): pl.pallas_call(adam_kernel, out_shape=outs, in_specs=[ANY] * 16 + [VMEM]...  16 us

profile of v4, /device:TPU:3, one launch (start us, length us, event | category | flops | bytes accessed | tf_op | source)
XLA Modules:
  0.0 355.9 jit_solution(4238837167348635777)
XLA Ops:
  0.7 0.0 copy-start.1
  0.7 0.9 reduce-window.8
  1.6 0.1 convert_reduce_fusion
  1.7 0.7 subtract_convert_fusion
  2.4 1.7 dynamic_update_slice.3.gain_in
  4.1 0.0 copy-start.3
  4.1 0.6 broadcast_in_dim.42.doc_queries.refs_20_
  4.8 1.8 convert_element_type.32.wo_in
  6.6 0.0 copy-done.3
  6.6 1.8 convert_element_type.35.wd_in
  8.4 0.0 copy-start
  8.4 1.0 broadcast_in_dim.41.doc_keys.refs_19_
  9.4 0.0 copy-done.1
  9.4 0.4 convert_element_type.33
  9.8 1.2 convert_element_type.34.wg_in
  11.0 0.0 copy-done
  11.0 0.5 reshape.107
  11.4 0.3 constant_dynamic-slice_fusion.1
  11.9 0.8 concatenate.9.wq_in
  12.7 1.9 fusion
  14.6 1.3 pad_maximum_fusion.1.sin_rows.refs_18_
  15.9 1.3 pad_maximum_fusion.cos_rows.refs_17_
  17.2 151.3 %forward.1 = (bf16[256,768]{1,0:T(8,128)(2,1)}, bf16[2,1024,768]{2,1,0:T(8,128)(2,1)}, bf16[2,1024,640]{2,1,0:T(8,128)(2,1)}, f32[2,8,1024]{2,1,0:T(8,128)}, bf1...) custom-call(bf16[256,768]{1,0:T(8,128)(2,1)} %tok.1, ...), custom_call_target="tpu_custom_call" | custom-call | flops 12000000000 | bytes 60000000 | tf_op jit(solution)/shard_map/forward/pallas_call | solution.py:1302
  168.5 166.9 %backward.1 = (f32[256,768]{1,0:T(8,128)}, bf16[2,4,96,640]{3,2,1,0:T(8,128)(2,1)}, bf16[2,2,96,384]{3,2,1,0:T(8,128)(2,1)}, f32[2,96,768]{2,1,0:T(8,128)}, f32[2,96,1536]{2,1,0:T(8,128)}, /*index=5*/f32[8,768]{1,0:T(8,128)}) custom-call(f32[256,768]{1,0:T(8,128)} %refs_0_.2, f32[2,256,768]{2,1,0:T(8,128)} %get-tuple-element.76.refs_1_, ...), custom_call_target="tpu_custom_call" | custom-call | flops 24000000000 | bytes 60000000 | tf_op jit(solution)/shard_map/backward/pallas_call | solution.py:1391
  335.4 0.7 slice.23
  336.1 0.7 constant_dynamic-slice_fusion.refs_24_
  336.8 0.0 copy-start.2
  336.8 16.0 %adam.1 = (f32[2,96,2304]{2,1,0:T(8,128)}, f32[2,96,2304]{2,1,0:T(8,128)}, f32[2,96,2304]{2,1,0:T(8,128)}, f32[2,96,2304]{2,1,0:T(8,128)}, f32[2,96,2304]{2,1,0:...) custom-call(f32[2,96,2304]{2,1,0:T(8,128)} %refs_0_.3, ...), custom_call_target="tpu_custom_call" | custom-call | flops 20000000 | bytes 37000000 | tf_op jit(solution)/shard_map/adam/pallas_call | solution.py:1429
  352.9 0.0 copy-done.2
  352.9 0.7 copy.66
  353.6 2.1 copy.67
  (7 shorter events, 0.1 us)
Async XLA Ops:
  0.7 8.7 %copy-start.1 = (f32[2,96,2,768]{3,2,1,0:T(2,128)S(1)}, f32[2,96,2,768]{3,2,1,0:T(2,128)}, u32[]{:S(2)}) copy-start(f32[2,96,2,768]{3,2,1,0:T(2,128)} %refs_8_.1) | copy-start | bytes 3538948
  4.1 2.4 copy-start.3
  8.4 2.6 copy-start
  336.8 16.1 %copy-start.2 = (bf16[256,768]{1,0:T(8,128)(2,1)S(1)}, bf16[256,768]{1,0:T(8,128)(2,1)}, u32[]{:S(2)}) copy-start(bf16[256,768]{1,0:T(8,128)(2,1)} %get-tuple-element.160) | copy-start | bytes 1179652
